TPU v7x, 256 devices: a whole 4x4x8 slice. The times are simulated.
256 devices in a mesh: rep: 8 (over y_lo, x), fsdp: 32 (over z, y_hi, core).
Axes of the slice: x: 4, y: 4 (y_hi: 2, y_lo: 2; y = y_hi * 2 + y_lo), z: 8, core: 2. Of those that a mesh axis runs over, the one named last changes fastest.
Arguments:
- activations: bfloat16 [8, 8192, 8192], P('rep', 'fsdp'), may hold values from -6 to 6
- weights: bfloat16 [8, 8192, 512], P('rep', 'fsdp'), may hold values from -6 to 6
- momentum: float32 [8, 8192, 512], P('rep', 'fsdp'), may hold values from -6 to 6
- cotangent: bfloat16 [8, 8192, 512], P('rep', 'fsdp'), may hold values from -6 to 6
- step_index: int32 [1], replicated, may hold values from 0 to 999
Outputs:
- values_out: bfloat16 [8, 8192, 512], P('rep', 'fsdp')
- input_grad: bfloat16 [8, 8192, 8192], P('rep', 'fsdp')
- new_weights: bfloat16 [8, 8192, 512], P('rep', 'fsdp')
- new_momentum: float32 [8, 8192, 512], P('rep', 'fsdp')
All inputs are finite; a program needn't handle non-finite values.
Results may differ from a plain program's by a relative error of at most 0.015.
Values may be sent and summed in bfloat16 or wider, within the bound.
No kernel may reach another device: no remote copies, remote signals or barrier semaphores. Data moves between devices by JAX's collectives and lax.ppermute only.
A program may use at most 128 MiB of HBM per device.

v0:
```python
from functools import partial

import jax
import jax.numpy as jnp
from jax import lax
from jax.sharding import PartitionSpec as P


def for_sending(shard):

    def short(part):
        return part.astype(jnp.bfloat16) if part.dtype == jnp.float32 else part

    return jax.tree.map(short, shard)


def from_partner(value, axis, apart):
    mask = 2**apart
    pairs = [(source, source ^ mask) for source in range(lax.axis_size(axis))]
    return lax.ppermute(value, axis, pairs)


def pair_with(payload, bit):
    return jax.tree.map(
        lambda part, own: part.astype(own.dtype),
        from_partner(for_sending(payload), "rep", bit),
        payload,
    )


def per_device(activations, weights, momentum, cotangent, step_index):
    acts = activations[0]
    cot = cotangent[0]
    weight = weights[0]
    width = acts.shape[1]
    scale = 1.0 / jnp.sqrt(jnp.float32(width))
    columns = acts
    total = jnp.dot(
        columns,
        lax.all_gather(weight, "fsdp", axis=0, tiled=True),
        preferred_element_type=jnp.float32,
    )
    ingrad = (
        lax.dot_general(
            cot,
            lax.all_gather(weight, "fsdp", axis=0, tiled=True),
            (((1,), (1,)), ((), ())),
            preferred_element_type=jnp.float32,
        )
        * scale
    ).astype(jnp.bfloat16)
    values = (total * scale).astype(jnp.bfloat16)
    columns = acts
    grad = lax.psum_scatter(
        (
            lax.dot_general(
                columns, cot, (((0,), (0,)), ((), ())), preferred_element_type=jnp.float32
            )
            * scale
        ).astype(jnp.bfloat16),
        "fsdp",
        scatter_dimension=0,
        tiled=True,
    ).astype(jnp.float32)
    step_float = step_index[0].astype(jnp.float32)
    rate = 0.1 * (0.5 + 0.5 * jnp.cos(jnp.float32(3.141592653589793) * step_float / 1000.0))
    moved = 0.9 * momentum[0] + grad
    stepped = (weight.astype(jnp.float32) - rate * moved).astype(jnp.bfloat16)
    bits = lax.axis_size("rep").bit_length() - 1
    branches = [partial(pair_with, bit=level) for level in range(bits)]
    bit_pick = step_index[0] % bits
    other_w, other_m = lax.switch(bit_pick, branches, (stepped.astype(jnp.float32), moved))
    new_w = ((stepped.astype(jnp.float32) + other_w) * 0.5).astype(jnp.bfloat16)
    new_m = (moved + other_m) * 0.5
    return (values[None], ingrad[None], new_w[None], new_m[None])


def solution(mesh):
    return jax.shard_map(
        per_device,
        mesh=mesh,
        in_specs=(
            P("rep", "fsdp", None),
            P("rep", "fsdp", None),
            P("rep", "fsdp", None),
            P("rep", "fsdp", None),
            P(),
        ),
        out_specs=(
            P("rep", "fsdp", None),
            P("rep", "fsdp", None),
            P("rep", "fsdp", None),
            P("rep", "fsdp", None),
        ),
        check_vma=False,
    )
```

profile of v0, /device:TPU:2, one launch (start us, length us, event | category | flops | bytes accessed | tf_op | source)
XLA Modules:
  0.0 294.6 jit_solution(12598563224317471509)
XLA Ops:
  7.2 0.0 copy-start
  7.2 0.0 reduce-scatter.2.cloned.1.call-start
  7.2 0.9 copy-done
  8.1 7.8 %multiply_convert_fusion = bf16[8192,512]{1,0:T(8,128)(2,1)} fusion(bf16[1,256,8192]{2,1,0:T(8,128)(2,1)} %param.8, bf16[1,256,512]{2,1,0:T(8,128)(2,1)S(1)} %copy-done), kind=kOutput, calls=%fused_computation | convolution fusion | flops 2155872256 | bytes 12845056 | tf_op jit(solution)/shard_map/dot_general | solution.py:56
  15.9 0.0 copy-start.1
  15.9 0.0 copy-start.2
  15.9 0.0 reduce-scatter.2.cloned.1.call-update
  16.0 0.0 all-gather.3.cloned.1.call-start
  16.0 0.7 all-gather.3.cloned.1.call-update
  17.4 155.9 %reduce-scatter.2.cloned.1.call-done = bf16[256,512]{1,0:T(8,128)(2,1)} async-done(((bf16[8192,512]{1,0:T(8,128)(2,1)}), bf16[256,512]{1,0:T(8,128)(2,1)}) %reduce-scatter.2.cloned.1.call-update) | async-done | bytes 262160 | tf_op jit(solution)/shard_map/reduce_scatter | solution.py:54
  173.3 0.0 copy-done.1
  173.3 0.0 copy-done.2
  173.3 1.1 fusion.24
  174.4 9.4 %conditional.4 = (f32[256,512]{1,0:T(8,128)S(1)}, f32[256,512]{1,0:T(8,128)S(1)}) conditional(s32[]{:T(128)} %clamp.3, (f32[256,512]{1,0:T(8,128)S(1)}, f32[256,512]{1,0:T(8,128)S(1)}) %fusion.24, (f32[256,512]{1,0:T(8,128)S(1)}, f32[256,512]{1,0:T(8,128)S(1)}) %fusion.24, (f32[256,512]{1,0:T(8,128)S(1)}, ...), branch_computations={%region_1.2_spmd, %region_2.3_spmd, %region_3.4_spmd} | conditional | flops 524288 | bytes 5242976
  174.5 0.7 collective-permute-start.5
  175.2 1.5 collective-permute-start.4
  176.7 4.2 %collective-permute-done.5 = bf16[256,512]{1,0:T(8,128)(2,1)S(1)} collective-permute-done((bf16[256,512]{1,0:T(8,128)(2,1)S(1)}, bf16[256,512]{1,0:T(8,128)(2,1)S(1)}, u32[]{:S(2)}, u32[]{:S(2)}) %collective-permute-start.5) | collective-permute-done | bytes 262176 | tf_op jit(solution)/shard_map/cond/branch_2_fun/ppermute | solution.py:20
  181.0 2.8 collective-permute-done.4
  183.8 1.1 multiply_bitcast_fusion
  184.9 90.6 %all-gather.3.cloned.1.call-done = bf16[1,8192,512]{2,1,0:T(8,128)(2,1)} async-done(((bf16[1,256,512]{2,1,0:T(8,128)(2,1)}), bf16[1,8192,512]{2,1,0:T(8,128)(2,1)}) %all-gather.3.cloned.1.call-update) | async-done | bytes 8388624 | tf_op jit(solution)/shard_map/all_gather | solution.py:40
  275.5 0.0 copy-start.3
  275.6 7.8 %fusion.17 = bf16[1,256,512]{2,1,0:T(8,128)(2,1)} fusion(bf16[1,8192,512]{2,1,0:T(8,128)(2,1)} %all-gather.3.cloned.1.call-done, bf16[1,256,8192]{2,1,0:T(8,128)(2,1)} %param.8), kind=kOutput, calls=%fused_computation.11 | convolution fusion | flops 2147745792 | bytes 12845056 | tf_op jit(solution)/shard_map/dot_general | solution.py:38
  283.4 0.0 copy-done.3
  283.4 4.4 %fusion.1 = bf16[1,256,8192]{2,1,0:T(8,128)(2,1)} fusion(bf16[1,8192,512]{2,1,0:T(8,128)(2,1)S(1)} %copy-done.3, bf16[1,256,512]{2,1,0:T(8,128)(2,1)S(1)} %copy-done), kind=kOutput, calls=%fused_computation.3 | convolution fusion | flops 2151677952 | bytes 12845056 | tf_op jit(solution)/shard_map/dot_general | solution.py:44
  (4 shorter events, 0.2 us)
Async XLA Ops:
  7.2 1.0 copy-start
  7.2 166.1 %reduce-scatter.2.cloned.1.call-start = ((), (), s32[]{:S(2)}) async-start(), calls=%async_computation.1 | async-start | bytes 8650752 | tf_op jit(solution)/shard_map/reduce_scatter | solution.py:54
  15.9 157.4 %copy-start.1 = (bf16[1,256,512]{2,1,0:T(8,128)(2,1)S(1)}, bf16[1,256,512]{2,1,0:T(8,128)(2,1)}, u32[]{:S(2)}) copy-start(bf16[1,256,512]{2,1,0:T(8,128)(2,1)} %param.9) | copy-start | bytes 786436
  15.9 157.4 %copy-start.2 = (f32[1,256,512]{2,1,0:T(8,128)S(1)}, f32[1,256,512]{2,1,0:T(8,128)}, u32[]{:S(2)}) copy-start(f32[1,256,512]{2,1,0:T(8,128)} %param.10) | copy-start | bytes 1572868
  16.0 259.6 %all-gather.3.cloned.1.call-start = ((), (), s32[]{:S(2)}) async-start(), calls=%async_computation.2 | async-start | bytes 8650752 | tf_op jit(solution)/shard_map/all_gather | solution.py:40
  174.5 6.5 %collective-permute-start.5 = (bf16[256,512]{1,0:T(8,128)(2,1)S(1)}, bf16[256,512]{1,0:T(8,128)(2,1)S(1)}, u32[]{:S(2)}, u32[]{:S(2)}) collective-permute-start(bf16[256,512]{1,0:T(8,128)(2,1)S(1)} %convert_element_type.70), channel_id=1, source_target_pairs={{0,128},{32,160},{64,192},{96,224},{128,0},{160,32},{192,64},{224,... | collective-permute-start | bytes 786440 | tf_op jit(solution)/shard_map/cond/branch_2_fun/ppermute | solution.py:20
  175.2 8.5 %collective-permute-start.4 = (bf16[256,512]{1,0:T(8,128)(2,1)S(1)}, bf16[256,512]{1,0:T(8,128)(2,1)S(1)}, u32[]{:S(2)}, u32[]{:S(2)}) collective-permute-start(bf16[256,512]{1,0:T(8,128)(2,1)S(1)} %convert_element_type.68), channel_id=1, source_target_pairs={{0,128},{32,160},{64,192},{96,224},{128,0},{160,32},{192,64},{224,... | collective-permute-start | bytes 786440 | tf_op jit(solution)/shard_map/cond/branch_2_fun/ppermute | solution.py:20
  275.5 7.8 %copy-start.3 = (bf16[1,8192,512]{2,1,0:T(8,128)(2,1)S(1)}, bf16[1,8192,512]{2,1,0:T(8,128)(2,1)}, u32[]{:S(2)}) copy-start(bf16[1,8192,512]{2,1,0:T(8,128)(2,1)} %all-gather.3.cloned.1.call-done) | copy-start | bytes 25165828
Sparse Core Ops, SparseCore 0:
  16.1 157.1 reduce-scatter.1
  176.1 99.4 all-gather.2
where the time goes:
time: 296 us; the launch traced here: 295 us
  waiting for transfers between devices  254 us (86%)
  matrix products  20 us (7%)
  between operations  14.8 us (5%)
    reduce_scatter x1, waiting for transfers between devices, per_device(): lax.psum_scatter((lax.dot_general(columns, cot, (((0,), (0,)), ((), ())),...  156 us
    all_gather x1, waiting for transfers between devices, per_device(): lax.all_gather(weight, 'fsdp', axis=0, tiled=True)  90.6 us
    dot_general x1, matrix products, per_device(): jnp.dot(columns, lax.all_gather(weight, 'fsdp', axis=0, tiled=True), pref...  7.82 us
    dot_general x1, matrix products, per_device(): lax.dot_general(columns, cot, (((0,), (0,)), ((), ())), preferred_element...  7.8 us
    ppermute x2, waiting for transfers between devices, from_partner(): return lax.ppermute(value, axis, pairs)  6.97 us
  transfers between devices with their start and end apart: 4, of which 4 were waited for; matrix products, arithmetic and copies ran while one was open for 1% of the time, Pallas kernels for 0%

commit v1 on v0

v1 whole, which is shorter than its diff:
```python
from functools import partial

import jax
import jax.numpy as jnp
from jax import lax
from jax.experimental import pallas as pl
from jax.experimental.pallas import tpu as pltpu
from jax.sharding import PartitionSpec as P

BF = jnp.bfloat16
F32 = jnp.float32
Z = 8
HALF = 128
SHARD = 256
KV = 512
ORDER = (4, 3, -3, 2, -2, 1, -1, 0)
MIB = 2**20
Y, CORE, PICK = 8, 9, 10
TOKEN = pl.BlockSpec((8, 128), lambda *_: (0, 0))
TOKEN_SHAPE = jax.ShapeDtypeStruct((8, 128), F32)


def send(value, move, axis="fsdp"):
    pairs = [(source, move(source)) for source in range(lax.axis_size(axis))]
    return lax.ppermute(value, axis, pairs)


def up(value):
    return send(value, lambda f: (f + 4) % 32)


def down(value):
    return send(value, lambda f: (f - 4) % 32)


def y_swap(value):
    return send(value, lambda f: f ^ 2)


def core_swap(value):
    return send(value, lambda f: f ^ 1)


def from_partner(value, *, bit):
    return send(value, lambda r: r ^ (1 << bit), "rep")


def params(mib):
    return pltpu.CompilerParams(vmem_limit_bytes=mib * MIB)


def cost(flops, bytes_accessed):
    return pl.CostEstimate(flops=flops // 1024, bytes_accessed=bytes_accessed // 1024, transcendentals=0)


def combine_kernel(*refs, outs):
    refs[-1][...] = jnp.zeros((8, 128), F32)
    for out, segments in zip(refs[-len(outs) - 1 : -1], outs, strict=True):
        at = 0
        for terms in segments:
            rows = terms[0][2]
            if len(terms) == 1:
                (source, start, _), = terms
                out[at : at + rows, :] = refs[source][start : start + rows, :]
            else:
                total = None
                for source, start, _ in terms:
                    part = refs[source][start : start + rows, :].astype(F32)
                    total = part if total is None else total + part
                out[at : at + rows, :] = total.astype(BF)
            at += rows


def combine(inputs, outs, after=()):
    specs, args = [], []
    for given in inputs:
        array, rows, index = given if isinstance(given, tuple) else (given, given.shape[0], 0)
        specs.append(pl.BlockSpec((rows, array.shape[1]), lambda i, index=index: (index, 0)))
        args.append(array)
    width = args[0].shape[1]
    specs += [TOKEN] * len(after)
    args += list(after)
    sizes = [sum(terms[0][2] for terms in segments) for segments in outs]
    shapes = [jax.ShapeDtypeStruct((rows, width), BF) for rows in sizes]
    return pl.pallas_call(
        partial(combine_kernel, outs=outs),
        grid=(1,),
        in_specs=specs,
        out_specs=[pl.BlockSpec(shape.shape, lambda i: (0, 0)) for shape in shapes] + [TOKEN],
        out_shape=shapes + [TOKEN_SHAPE],
        compiler_params=params(16),
        cost_estimate=cost(0, 4 * width * sum(sizes)),
    )(*args)


def choose_kernel(where, *refs):
    *found, out, token = refs
    token[...] = jnp.zeros((8, 128), F32)
    for bit, given in enumerate(found):

        @pl.when(where[PICK] == bit)
        def _(given=given):
            out[...] = given[...]


def choose(where, found):
    whole = pl.BlockSpec((SHARD, KV), lambda i, p: (0, 0))
    return pl.pallas_call(
        choose_kernel,
        grid_spec=pltpu.PrefetchScalarGridSpec(
            num_scalar_prefetch=1,
            grid=(1,),
            in_specs=[whole] * len(found),
            out_specs=[whole, TOKEN],
        ),
        out_shape=[jax.ShapeDtypeStruct((SHARD, KV), BF), TOKEN_SHAPE],
        compiler_params=params(8),
        cost_estimate=cost(0, MIB),
    )(where, *found)


def prep_kernel(where, rate, acts, mine, give):
    y, core = where[Y], where[CORE]
    for k in range(2):
        y_at = lax.rem(y + k, 2)
        to = slice(k * SHARD, (k + 1) * SHARD)
        own = pl.multiple_of((y_at * 2 + core) * SHARD, SHARD)
        sib = pl.multiple_of((y_at * 2 + 1 - core) * SHARD, SHARD)
        mine[:, to] = acts[:, pl.ds(own, SHARD)]
        give[:, to] = acts[:, pl.ds(sib, SHARD)]


def prep(where, rate, acts):
    half = jax.ShapeDtypeStruct((SHARD, 4096), BF)
    return pl.pallas_call(
        prep_kernel,
        grid_spec=pltpu.PrefetchScalarGridSpec(
            num_scalar_prefetch=2,
            grid=(Z,),
            in_specs=[pl.BlockSpec((SHARD, 1024), lambda i, w, _: (0, w[i]))],
            out_specs=[pl.BlockSpec((SHARD, 512), lambda i, *_: (0, i))] * 2,
        ),
        out_shape=[half, half],
        compiler_params=params(8),
        cost_estimate=cost(0, 8 * MIB),
    )(where, rate, acts)


def partials_kernel(mine, got, cot, got_cot, first, second, third, local, token, turned, *, scale):
    step = pl.program_id(0)
    token[...] = jnp.zeros((8, 128), F32)

    @pl.when(step == 0)
    def _():
        turned[:, :SHARD] = cot[...].T
        turned[:, SHARD:] = got_cot[...].T

    total = jnp.dot(turned[:, :SHARD], mine[...], preferred_element_type=F32)
    total += jnp.dot(turned[:, SHARD:], got[...], preferred_element_type=F32)
    total = (total * scale).astype(BF)
    own_a, own_b, other_a, other_b = (total[:, k * HALF : (k + 1) * HALF] for k in range(4))
    local[0:KV, :] = own_a
    local[KV : 2 * KV, :] = own_b
    local[2 * KV :, :] = other_b

    @pl.when(step == 0)
    def _():
        first[0:KV, :] = other_a
        first[KV : 2 * KV, :] = other_b

    for i in range(1, Z):

        @pl.when(step == i)
        def _(i=i):
            out, at = (second, i - 1) if i < 3 else (third, i - 3)
            out[at * KV : (at + 1) * KV, :] = other_a


def partials(mine, got, cot, got_cot, scale):
    columns = pl.BlockSpec((SHARD, 512), lambda i: (0, i))
    held = pl.BlockSpec((SHARD, KV), lambda i: (0, 0))
    sizes = (2 * KV, 2 * KV, 5 * KV)
    return pl.pallas_call(
        partial(partials_kernel, scale=scale),
        grid=(Z,),
        in_specs=[columns, columns, held, held],
        out_specs=[pl.BlockSpec((rows, HALF), lambda i: (0, 0)) for rows in sizes]
        + [pl.BlockSpec((3 * KV, HALF), lambda i: (i, 0)), TOKEN],
        out_shape=[jax.ShapeDtypeStruct((rows, HALF), BF) for rows in sizes + (Z * 3 * KV,)] + [TOKEN_SHAPE],
        scratch_shapes=[pltpu.VMEM((KV, 512), BF)],
        compiler_params=params(16),
        cost_estimate=cost(2 * 4096 * 512 * 512, 9 * MIB),
    )(mine, got, cot, got_cot)


def products_kernel(*refs, plan, n_pieces, first, last, scale):
    pieces = refs[:n_pieces]
    mine, got, cot, got_cot, _, *rest = refs[n_pieces:]
    if not first:
        total_in, *rest = rest
    step = pl.program_id(0)
    block = rest[-1]
    rest[-2][...] = jnp.zeros((8, 128), F32)
    for i, entry in enumerate(plan):

        @pl.when(step == i)
        def _(entry=entry):
            at = 0
            for piece, start, rows in entry:
                block[at : at + rows, :] = pieces[piece][start : start + rows, :]
                at += rows

    across = (((1,), (1,)), ((), ()))
    here = (lax.dot_general(cot[...], block[...], across, preferred_element_type=F32) * scale).astype(BF)
    there = (lax.dot_general(got_cot[...], block[...], across, preferred_element_type=F32) * scale).astype(BF)
    own = jnp.dot(mine[...], block[...], preferred_element_type=F32)
    sib = jnp.dot(got[...], block[...], preferred_element_type=F32)
    if last:
        in_here, total, tail, token, _ = rest
        in_here[...] = here
        tail[:, :512] = there
        total[...] = total_in[:SHARD, :] + own
        tail[:, 512:] = (total_in[SHARD:, :] + sib).astype(BF)
        return
    in_here, in_there, total, token, _ = rest
    in_here[...] = here
    in_there[...] = there

    @pl.when(step == 0)
    def _():
        if first:
            total[:SHARD, :] = own
            total[SHARD:, :] = sib
        else:
            total[:SHARD, :] = total_in[:SHARD, :] + own
            total[SHARD:, :] = total_in[SHARD:, :] + sib

    @pl.when(step > 0)
    def _():
        total[:SHARD, :] += own
        total[SHARD:, :] += sib


def products(base, plan, pieces, mine, got, cot, got_cot, total, scale, after, last=False):
    n = len(plan)
    whole = lambda a: pl.BlockSpec(a.shape, lambda i: (0, 0))
    columns = pl.BlockSpec((SHARD, 512), lambda i: (0, base + i))
    out_columns = pl.BlockSpec((SHARD, 512), lambda i: (0, i))
    args = list(pieces) + [mine, got, cot, got_cot, after]
    in_specs = [whole(p) for p in pieces] + [columns, columns, whole(cot), whole(cot), TOKEN]
    if total is not None:
        args.append(total)
        in_specs.append(whole(total))
    wide = jax.ShapeDtypeStruct((SHARD, 512 * n), BF)
    if last:
        shapes = [wide, jax.ShapeDtypeStruct((SHARD, KV), F32), jax.ShapeDtypeStruct((SHARD, 1024), BF)]
        out_specs = [out_columns, whole(shapes[1]), whole(shapes[2]), TOKEN]
    else:
        shapes = [wide, wide, jax.ShapeDtypeStruct((512, KV), F32)]
        out_specs = [out_columns, out_columns, whole(shapes[2]), TOKEN]
    return pl.pallas_call(
        partial(products_kernel, plan=plan, n_pieces=len(pieces), first=total is None, last=last, scale=scale),
        grid=(n,),
        in_specs=in_specs,
        out_specs=out_specs,
        out_shape=shapes + [TOKEN_SHAPE],
        scratch_shapes=[pltpu.VMEM((512, KV), BF)],
        compiler_params=params(20),
        cost_estimate=cost(n * 8 * SHARD * 512 * 512, (n + 4) * MIB),
    )(*args)


def place_kernel(where, own, sib, *rest):
    out = rest[-1]
    y, core = where[Y], where[CORE]
    for k in range(2):
        y_at = lax.rem(y + k, 2)
        part = slice(k * SHARD, (k + 1) * SHARD)
        out[:, pl.ds(pl.multiple_of((y_at * 2 + core) * SHARD, SHARD), SHARD)] = own[:, part]
        out[:, pl.ds(pl.multiple_of((y_at * 2 + 1 - core) * SHARD, SHARD), SHARD)] = sib[:, part]


def place_last_kernel(where, own, sib, total, _, out, values, *, scale):
    place_kernel(where, own, sib, out)
    values[...] = ((total[...] + sib[:, 512:].astype(F32)) * scale).astype(BF)


def place(where, base, own, sib, into, total=None, scale=None):
    n = own.shape[1] // 512
    columns = pl.BlockSpec((SHARD, 512), lambda i, w: (0, i))
    held = pl.BlockSpec((SHARD, KV), lambda i, w: (0, 0))
    args, specs, aliases = [own, sib], [columns, columns], {}
    out_specs = [pl.BlockSpec((SHARD, 1024), lambda i, w: (0, w[base + i]))]
    shapes = [jax.ShapeDtypeStruct((SHARD, 8192), BF)]
    kernel = place_kernel
    if total is not None:
        kernel = partial(place_last_kernel, scale=scale)
        args.append(total)
        specs = [columns, pl.BlockSpec((SHARD, 1024), lambda i, w: (0, 0)), held]
        out_specs.append(held)
        shapes.append(jax.ShapeDtypeStruct((SHARD, KV), BF))
    if into is not None:
        args.append(into)
        specs.append(pl.BlockSpec(memory_space=pl.ANY))
        aliases = {len(args): 0}
    return pl.pallas_call(
        kernel,
        grid_spec=pltpu.PrefetchScalarGridSpec(
            num_scalar_prefetch=1, grid=(n,), in_specs=specs, out_specs=out_specs
        ),
        out_shape=shapes,
        input_output_aliases=aliases,
        compiler_params=params(8),
        cost_estimate=cost(0, n * MIB),
    )(where, *args)


def moved_kernel(local, from_y, su, sd, yf, momentum, moved, short):
    def add(*parts):
        total = parts[0].astype(F32)
        for part in parts[1:]:
            total = total + part.astype(F32)
        return total.T

    low = add(local[0:KV, :], from_y[...], su[0:KV, :], sd[0:KV, :])
    high = add(local[KV : 2 * KV, :], su[KV:, :], sd[KV:, :], yf[...])
    new_low = 0.9 * momentum[0:HALF, :] + low
    new_high = 0.9 * momentum[HALF:, :] + high
    moved[0:HALF, :] = new_low
    moved[HALF:, :] = new_high
    short[0:HALF, :] = new_low.astype(BF)
    short[HALF:, :] = new_high.astype(BF)


def move(local, from_y, su, sd, yf, momentum):
    whole = lambda rows, cols, index=0: pl.BlockSpec((rows, cols), lambda i: (index, 0))
    return pl.pallas_call(
        moved_kernel,
        grid=(1,),
        in_specs=[
            whole(3 * KV, HALF, Z - 1),
            whole(KV, HALF, 4),
            whole(2 * KV, HALF),
            whole(2 * KV, HALF),
            whole(KV, HALF),
            whole(SHARD, KV),
        ],
        out_specs=[whole(SHARD, KV), whole(SHARD, KV)],
        out_shape=[jax.ShapeDtypeStruct((SHARD, KV), F32), jax.ShapeDtypeStruct((SHARD, KV), BF)],
        compiler_params=params(16),
        cost_estimate=cost(0, 3 * MIB),
    )(local, from_y, su, sd, yf, momentum)


def average_kernel(where, rate, weight, moved, other_w, found, new_w, new_m):
    def step(given, by):
        return (given.astype(F32) - rate[0] * by).astype(BF).astype(F32)

    other_m = found[0][...]
    for bit in range(1, len(found)):
        other_m = jnp.where(where[PICK] == bit, found[bit][...], other_m)
    other_m = other_m.astype(F32)
    new_m[...] = (moved[...] + other_m) * 0.5
    new_w[...] = ((step(weight[...], moved[...]) + step(other_w[...], other_m)) * 0.5).astype(BF)


def average(where, rate, weight, moved, other_w, found):
    def kernel(where, rate, weight, moved, other_w, *rest):
        average_kernel(where, rate, weight, moved, other_w, rest[:-2], *rest[-2:])

    rows = pl.BlockSpec((HALF, KV), lambda i, *_: (i, 0))
    return pl.pallas_call(
        kernel,
        grid_spec=pltpu.PrefetchScalarGridSpec(
            num_scalar_prefetch=2,
            grid=(SHARD // HALF,),
            in_specs=[rows] * (3 + len(found)),
            out_specs=[rows, rows],
        ),
        out_shape=[jax.ShapeDtypeStruct((SHARD, KV), BF), jax.ShapeDtypeStruct((SHARD, KV), F32)],
        compiler_params=params(8),
        cost_estimate=cost(0, 3 * MIB),
    )(where, rate, weight, moved, other_w, *found)


def per_device(activations, weights, momentum, cotangent, step_index):
    acts, cot, w = activations[0], cotangent[0], weights[0]
    scale = 1.0 / (8192.0**0.5)
    me = lax.axis_index("fsdp")
    z, y, core = me // 4, (me // 2) % 2, me % 2

    bits = lax.axis_size("rep").bit_length() - 1
    step_float = step_index.astype(F32)
    rate = 0.1 * (0.5 + 0.5 * jnp.cos(jnp.float32(3.141592653589793) * step_float / 1000.0))
    where = jnp.stack([(z + d + Z) % Z for d in ORDER] + [y, core, step_index[0] % bits]).astype(jnp.int32)

    found = [from_partner(w, bit=bit) for bit in range(bits)]
    other_w, t_w = choose(where, found)

    u1, d1, y0 = up(w), down(w), y_swap(w)

    mine, give = prep(where, rate, acts)
    got, got_cot = core_swap(give), core_swap(cot)

    to_y0, to_y1, to_y2, local, t_part = partials(mine, got, cot, got_cot, scale)

    pay_u, pay_d, pay_y, _ = combine(
        [u1, d1, y0],
        [
            [[(0, HALF, HALF)], [(0, 0, HALF)], [(2, HALF, HALF)]],
            [[(1, 0, SHARD)], [(2, HALF, HALF)]],
            [[(0, 0, HALF)], [(1, 0, HALF)]],
        ]
    )
    u2, d2, y1 = up(pay_u), down(pay_d), y_swap(pay_y)
    from_y0, from_y1, from_y2 = y_swap(to_y0), y_swap(to_y1), y_swap(to_y2)

    def loc(i):
        return (local, 3 * KV, i)

    own, own_high, other = 0, KV, 2 * KV
    pay_u, pay_d, t_s1 = combine(
        [loc(0), loc(1), loc(2), from_y0],
        [
            [[(0, own, KV), (3, 0, KV)], [(1, other, KV)]],
            [[(0, own_high, KV), (3, KV, KV)], [(2, other, KV)]],
        ],
    )
    su1, sd1 = up(pay_u), down(pay_d)

    pay_y, _ = combine([u2, d2], [[[(0, HALF, HALF)], [(1, 0, HALF)]]])
    u3, d3, y2 = up(u2), down(d2), y_swap(pay_y)

    total = None
    ing1, give1, total, t_g1 = products(
        5,
        (
            ((1, 0, SHARD), (3, HALF, HALF), (5, 2 * HALF, HALF)),
            ((0, 0, SHARD), (3, 0, HALF), (4, 2 * HALF, HALF)),
            ((6, 0, SHARD), (2, 0, SHARD)),
        ),
        (u1, d1, y0, y1, u2, d2, w),
        mine, got, cot, got_cot, None, scale, t_part,
    )
    got1 = core_swap(give1)

    pay_u, pay_d, t_s2 = combine(
        [loc(1), loc(2), loc(3), loc(4), (from_y1, KV, 0), (from_y1, KV, 1), su1, sd1],
        [
            [[(0, own, KV), (4, 0, KV), (6, 0, KV)], [(0, own_high, KV)], [(2, other, KV), (6, KV, KV)]],
            [[(1, own, KV), (5, 0, KV)], [(1, own_high, KV), (7, 0, KV)], [(3, other, KV), (7, KV, KV)]],
        ],
    )
    su2, sd2 = up(pay_u), down(pay_d)

    pay_u, pay_d, pay_y, _ = combine(
        [u3, d3],
        [[[(0, HALF, SHARD)]], [[(1, HALF, SHARD)]], [[(0, HALF, HALF)], [(1, 0, HALF)]]]
    )
    u4, d4, y3 = up(pay_u), down(pay_d), y_swap(pay_y)
    ing2, give2, total, t_g2 = products(
        3,
        (
            ((1, 0, SHARD), (2, HALF, HALF), (4, SHARD, HALF)),
            ((0, HALF, HALF), (0, 0, HALF), (2, 0, HALF), (3, SHARD, HALF)),
        ),
        (u2, d2, y2, u3, d3),
        mine, got, cot, got_cot, total, scale, t_part,
    )
    got2 = core_swap(give2)

    def third(own_at, y_at, other_at, got_at):
        return [
            [(own_at, own, KV), (y_at, 0, KV), (got_at, 0, KV)],
            [(own_at, own_high, KV), (got_at, KV, KV)],
            [(other_at, other, KV), (got_at, 2 * KV, KV)],
        ]

    pay_u, pay_d, t_s3 = combine(
        [loc(3), loc(4), loc(5), loc(6), (from_y2, KV, 0), (from_y2, KV, 1), su2, sd2],
        [third(0, 4, 2, 6), third(1, 5, 3, 7)]
    )
    su3, sd3 = up(pay_u), down(pay_d)

    pay_u, pay_d, pay_y, t_s4 = combine(
        [loc(5), loc(6), loc(7), (from_y2, KV, 2), (from_y2, KV, 3), su3, sd3],
        [
            [[(0, own, KV), (3, 0, KV), (5, 0, KV)], [(0, own_high, KV), (5, KV, KV)]],
            [[(1, own, KV), (4, 0, KV), (6, 0, KV)], [(1, own_high, KV), (6, KV, KV)]],
            [[(2, other, KV), (5, 2 * KV, KV), (6, 2 * KV, KV)]],
        ]
    )
    su4, sd4, yf = up(pay_u), down(pay_d), y_swap(pay_y)

    pay_y, _ = combine([u4, d4], [[[(0, 0, HALF)], [(1, 0, HALF)]]])
    y4 = y_swap(pay_y)
    ing3, give3, total, t_g3 = products(
        1,
        (
            ((1, 0, SHARD), (2, HALF, HALF), (4, HALF, HALF)),
            ((0, HALF, HALF), (0, 0, HALF), (2, 0, HALF), (3, HALF, HALF)),
        ),
        (u3, d3, y3, u4, d4),
        mine, got, cot, got_cot, total, scale, t_part,
    )
    got3 = core_swap(give3)

    ing4, total, tail, _ = products(
        0,
        (((0, 0, HALF), (1, 0, HALF), (2, 0, SHARD)),),
        (u4, d4, y4),
        mine, got, cot, got_cot, total, scale, t_part, last=True,
    )
    got4 = core_swap(tail)

    moved, short = move(local, from_y2, su4, sd4, yf, momentum[0])
    found = [from_partner(short, bit=bit) for bit in range(bits)]
    new_w, new_m = average(where, rate, w, moved, other_w, found)

    (ingrad,) = place(where, 5, ing1, got1, None)
    (ingrad,) = place(where, 3, ing2, got2, ingrad)
    (ingrad,) = place(where, 1, ing3, got3, ingrad)
    ingrad, values = place(where, 0, ing4, got4, ingrad, total, scale)
    return (values[None], ingrad[None], new_w[None], new_m[None])


def solution(mesh):
    rows = P("rep", "fsdp", None)
    return jax.shard_map(
        per_device,
        mesh=mesh,
        in_specs=(rows, rows, rows, rows, P()),
        out_specs=(rows, rows, rows, rows),
        check_vma=False,
    )
```

time: 296 us -> 123 us (0.42)
  waiting for transfers between devices: 254 us -> 35.8 us
  starting transfers between devices: 2.28 us -> 52 us
  Pallas kernels: 0 us -> 31.6 us
  matrix products: 20 us -> 0 us
  between operations: 14.8 us -> 1.66 us
    reduce_scatter x1 -> x0, waiting for transfers between devices: 156 us -> none  [per_device(): lax.psum_scatter((lax.dot_general(columns, cot, (((0,), (0,)), ((), ())),...]
    all_gather x1 -> x0, waiting for transfers between devices: 90.6 us -> none  [per_device(): lax.all_gather(weight, 'fsdp', axis=0, tiled=True)]
    ppermute x2 -> x37, starting transfers between devices: 2.2 us -> 52 us  [send(): return lax.ppermute(value, axis, pairs)]
    pallas_call x0 -> x21, Pallas kernels: none -> 31.6 us  [the longest x4 9.78 us: products(): pl.pallas_call(partial(products_kernel, plan=plan, n_pieces=len(pieces),...]
    ppermute x2 -> x37, waiting for transfers between devices: 6.97 us -> 35.8 us  [send(): return lax.ppermute(value, axis, pairs)]
    dot_general x3 -> x0, matrix products: 20 us -> none  [the longest x1 7.82 us: per_device(): jnp.dot(columns, lax.all_gather(weight, 'fsdp', axis=0, tiled=True), pref...]
  transfers between devices with their start and end apart: 4 -> 37, of which waited for: 4 -> 12; matrix products, arithmetic and copies ran while one was open for 1% -> 0% of each run, Pallas kernels for 0% -> 23%
where the time goes in v1:
time: 123 us
  starting transfers between devices  52 us (42%)
  waiting for transfers between devices  35.8 us (29%)
  Pallas kernels  31.6 us (26%)
  local copies, waits for them, and re-layouts  2.29 us (2%)
  between operations  1.66 us (1%)
    ppermute x37, starting transfers between devices, send(): return lax.ppermute(value, axis, pairs)  52 us
    ppermute x37, waiting for transfers between devices, send(): return lax.ppermute(value, axis, pairs)  35.8 us
    pallas_call x4, Pallas kernels, products(): pl.pallas_call(partial(products_kernel, plan=plan, n_pieces=len(pieces),...  9.78 us
    pallas_call x4, Pallas kernels, place(): pl.pallas_call(kernel, grid_spec=pltpu.PrefetchScalarGridSpec(num_scalar_...  7.28 us
    pallas_call x8, Pallas kernels, combine(): pl.pallas_call(partial(combine_kernel, outs=outs), grid=(1,), in_specs=sp...  5.14 us
    pallas_call x1, Pallas kernels, partials(): pl.pallas_call(partial(partials_kernel, scale=scale), grid=(Z,), in_specs...  4.54 us
  transfers between devices with their start and end apart: 37, of which 12 were waited for; matrix products, arithmetic and copies ran while one was open for 0% of the time, Pallas kernels for 23%

profile of v1, /device:TPU:2, one launch (start us, length us, event | category | flops | bytes accessed | tf_op | source)
XLA Modules:
  0.0 123.3 jit_solution(5228474111152458705)
XLA Ops:
  1.7 2.2 %copy-done.1 = bf16[1,256,8192]{2,1,0:T(8,128)(2,1)S(1)} copy-done((bf16[1,256,8192]{2,1,0:T(8,128)(2,1)S(1)}, bf16[1,256,8192]{2,1,0:T(8,128)(2,1)}, u32[]{:S(2)}) %copy-start.1) | copy-done | bytes 4194328
  3.8 1.9 %shard_map.87 = (bf16[256,4096]{1,0:T(8,128)(2,1)S(1)}, bf16[256,4096]{1,0:T(8,128)(2,1)S(1)}) custom-call(s32[11]{0:T(128)S(1)} %stack.47.where, f32[1]{0:T(128)S(6)} %mul.8.rate, bf16[256,8192]{1,0:T(8,128)(2,1)S(1)} %bitcast.26), custom_call_target="tpu_custom_call" | custom-call | bytes 8192 | tf_op jit(solution)/shard_map/pallas_call | solution.py:135
  6.3 3.2 %collective-permute-start.2 = (bf16[256,512]{1,0:T(8,128)(2,1)S(1)}, bf16[256,512]{1,0:T(8,128)(2,1)S(1)}, u32[]{:S(2)}, u32[]{:S(2)}) collective-permute-start(bf16[256,512]{1,0:T(8,128)(2,1)S(1)} %bitcast.27), channel_id=1, source_target_pairs={{0,2},{1,3},{2,0},{3,1},{4,6},{5,7},{6,4},{7,5},{8,10},{9,11},{10,... | collective-permute-start | bytes 786440 | tf_op jit(solution)/shard_map/ppermute | solution.py:25
  9.5 5.9 %collective-permute-start.1 = (bf16[256,512]{1,0:T(8,128)(2,1)S(1)}, bf16[256,512]{1,0:T(8,128)(2,1)S(1)}, u32[]{:S(2)}, u32[]{:S(2)}) collective-permute-start(bf16[256,512]{1,0:T(8,128)(2,1)S(1)} %bitcast.28), channel_id=1, source_target_pairs={{0,28},{1,29},{2,30},{3,31},{4,0},{5,1},{6,2},{7,3},{8,4},{9,5},{1... | collective-permute-start | bytes 786440 | tf_op jit(solution)/shard_map/ppermute | solution.py:25
  15.4 4.5 %shard_map.88 = (bf16[1024,128]{1,0:T(8,128)(2,1)S(1)}, bf16[1024,128]{1,0:T(8,128)(2,1)S(1)}, bf16[2560,128]{1,0:T(8,128)(2,1)S(1)}, bf16[12288,128]{1,0:T(8,128)(2,1)S(1)}, f32[8,128]{1,0:T(8,128)S(1)}) custom-call(bf16[256,4096]{1,0:T(8,128)(2,1)S(1)} %get-tuple-element.52.mine.refs_7_.refs_5_.refs_3_, ...), custom_call_target="tpu_custom_call" | custom-call | flops 2097152 | bytes 9216 | tf_op jit(solution)/shard_map/pallas_call | solution.py:183
  20.4 3.2 %collective-permute-start.20 = (bf16[1024,128]{1,0:T(8,128)(2,1)S(1)}, bf16[1024,128]{1,0:T(8,128)(2,1)S(1)}, u32[]{:S(2)}, u32[]{:S(2)}) collective-permute-start(bf16[1024,128]{1,0:T(8,128)(2,1)S(1)} %get-tuple-element.74), channel_id=1, source_target_pairs={{0,2},{1,3},{2,0},{3,1},{4,6},{5,7},{6,4},{7,5},{8,10},{9,11},{10,... | collective-permute-start | bytes 786440 | tf_op jit(solution)/shard_map/ppermute | solution.py:25
  24.3 0.7 shard_map.84
  25.0 3.2 %collective-permute-start.5 = (bf16[384,512]{1,0:T(8,128)(2,1)S(1)}, bf16[384,512]{1,0:T(8,128)(2,1)S(1)}, u32[]{:S(2)}, u32[]{:S(2)}) collective-permute-start(bf16[384,512]{1,0:T(8,128)(2,1)S(1)} %get-tuple-element.48), channel_id=1, source_target_pairs={{0,28},{1,29},{2,30},{3,31},{4,0},{5,1},{6,2},{7,3},{8,4},{9,5},{1... | collective-permute-start | bytes 1179656 | tf_op jit(solution)/shard_map/ppermute | solution.py:25
  28.2 2.5 %collective-permute-done.21.refs_3_ = bf16[1024,128]{1,0:T(8,128)(2,1)S(1)} collective-permute-done((bf16[1024,128]{1,0:T(8,128)(2,1)S(1)}, bf16[1024,128]{1,0:T(8,128)(2,1)S(1)}, u32[]{:S(2)}, u32[]{:S(2)}) %collective-permute-start.21) | collective-permute-done | bytes 262176 | tf_op jit(solution)/shard_map/ppermute | solution.py:25
  31.4 5.0 %collective-permute-done.20.refs_4_.refs_5_ = bf16[1024,128]{1,0:T(8,128)(2,1)S(1)} collective-permute-done((bf16[1024,128]{1,0:T(8,128)(2,1)S(1)}, bf16[1024,128]{1,0:T(8,128)(2,1)S(1)}, u32[]{:S(2)}, u32[]{:S(2)}) %collective-permute-start.20) | collective-permute-done | bytes 262176 | tf_op jit(solution)/shard_map/ppermute | solution.py:25
  36.4 3.2 %collective-permute-start.23 = (bf16[1024,128]{1,0:T(8,128)(2,1)S(1)}, bf16[1024,128]{1,0:T(8,128)(2,1)S(1)}, u32[]{:S(2)}, u32[]{:S(2)}) collective-permute-start(bf16[1024,128]{1,0:T(8,128)(2,1)S(1)} %get-tuple-element.77), channel_id=1, source_target_pairs={{0,28},{1,29},{2,30},{3,31},{4,0},{5,1},{6,2},{7,3},{8,4},{9,5},{1... | collective-permute-start | bytes 786440 | tf_op jit(solution)/shard_map/ppermute | solution.py:25
  39.6 2.8 %collective-permute-done.22.refs_6_ = bf16[1024,128]{1,0:T(8,128)(2,1)S(1)} collective-permute-done((bf16[1024,128]{1,0:T(8,128)(2,1)S(1)}, bf16[1024,128]{1,0:T(8,128)(2,1)S(1)}, u32[]{:S(2)}, u32[]{:S(2)}) %collective-permute-start.22) | collective-permute-done | bytes 262176 | tf_op jit(solution)/shard_map/ppermute | solution.py:25
  42.4 1.1 collective-permute-done.23.refs_7_
  43.5 0.6 shard_map.99
  44.2 3.7 %collective-permute-start.25 = (bf16[1536,128]{1,0:T(8,128)(2,1)S(1)}, bf16[1536,128]{1,0:T(8,128)(2,1)S(1)}, u32[]{:S(2)}, u32[]{:S(2)}) collective-permute-start(bf16[1536,128]{1,0:T(8,128)(2,1)S(1)} %get-tuple-element.79), channel_id=1, source_target_pairs={{0,28},{1,29},{2,30},{3,31},{4,0},{5,1},{6,2},{7,3},{8,4},{9,5},{1... | collective-permute-start | bytes 1179656 | tf_op jit(solution)/shard_map/ppermute | solution.py:25
  47.9 3.2 %collective-permute-start.6 = (bf16[384,512]{1,0:T(8,128)(2,1)S(1)}, bf16[384,512]{1,0:T(8,128)(2,1)S(1)}, u32[]{:S(2)}, u32[]{:S(2)}) collective-permute-start(bf16[384,512]{1,0:T(8,128)(2,1)S(1)} %collective-permute-done.5.refs_1_.refs_5_), channel_id=1, source_target_pairs={{0,28},{1,29},{2,30},{3,31},{4,0},{5,1},{6,2},{7,3},{8,4},{9,5},{1... | collective-permute-start | bytes 1179656 | tf_op jit(solution)/shard_map/ppermute | solution.py:25
  51.1 0.7 collective-permute-start.33
  51.8 6.1 %collective-permute-done.24.refs_6_ = bf16[1536,128]{1,0:T(8,128)(2,1)S(1)} collective-permute-done((bf16[1536,128]{1,0:T(8,128)(2,1)S(1)}, bf16[1536,128]{1,0:T(8,128)(2,1)S(1)}, u32[]{:S(2)}, u32[]{:S(2)}) %collective-permute-start.24) | collective-permute-done | bytes 393248 | tf_op jit(solution)/shard_map/ppermute | solution.py:25
  57.9 0.7 shard_map.100
  58.6 0.9 collective-permute-start.26
  59.5 0.7 collective-permute-start.14
  60.2 6.1 %collective-permute-done.4.refs_0_.refs_3_ = bf16[384,512]{1,0:T(8,128)(2,1)S(1)} collective-permute-done((bf16[384,512]{1,0:T(8,128)(2,1)S(1)}, bf16[384,512]{1,0:T(8,128)(2,1)S(1)}, u32[]{:S(2)}, u32[]{:S(2)}) %collective-permute-start.4) | collective-permute-done | bytes 393248 | tf_op jit(solution)/shard_map/ppermute | solution.py:25
  66.3 2.0 %collective-permute-start.27 = (bf16[1536,128]{1,0:T(8,128)(2,1)S(1)}, bf16[1536,128]{1,0:T(8,128)(2,1)S(1)}, u32[]{:S(2)}, u32[]{:S(2)}) collective-permute-start(bf16[1536,128]{1,0:T(8,128)(2,1)S(1)} %get-tuple-element.81), channel_id=1, source_target_pairs={{0,28},{1,29},{2,30},{3,31},{4,0},{5,1},{6,2},{7,3},{8,4},{9,5},{1... | collective-permute-start | bytes 1179656 | tf_op jit(solution)/shard_map/ppermute | solution.py:25
  69.0 3.2 %collective-permute-start.8 = (bf16[256,512]{1,0:T(8,128)(2,1)S(1)}, bf16[256,512]{1,0:T(8,128)(2,1)S(1)}, u32[]{:S(2)}, u32[]{:S(2)}) collective-permute-start(bf16[256,512]{1,0:T(8,128)(2,1)S(1)} %get-tuple-element.50), channel_id=1, source_target_pairs={{0,28},{1,29},{2,30},{3,31},{4,0},{5,1},{6,2},{7,3},{8,4},{9,5},{1... | collective-permute-start | bytes 786440 | tf_op jit(solution)/shard_map/ppermute | solution.py:25
  72.8 2.1 %collective-permute-start.32 = (bf16[256,512]{1,0:T(8,128)(2,1)S(1)}, bf16[256,512]{1,0:T(8,128)(2,1)S(1)}, u32[]{:S(2)}, u32[]{:S(2)}) collective-permute-start(bf16[256,512]{1,0:T(8,128)(2,1)S(1)} %bitcast.31), channel_id=1, source_target_pairs={{0,64},{32,96},{64,0},{96,32},{128,192},{160,224},{192,128},{224,1... | collective-permute-start | bytes 786440 | tf_op jit(solution)/shard_map/ppermute | solution.py:25
  75.0 1.6 %collective-permute-done.7.refs_0_.refs_3_ = bf16[256,512]{1,0:T(8,128)(2,1)S(1)} collective-permute-done((bf16[256,512]{1,0:T(8,128)(2,1)S(1)}, bf16[256,512]{1,0:T(8,128)(2,1)S(1)}, u32[]{:S(2)}, u32[]{:S(2)}) %collective-permute-start.7) | collective-permute-done | bytes 262176 | tf_op jit(solution)/shard_map/ppermute | solution.py:25
  76.6 1.6 %collective-permute-start.13 = (bf16[256,512]{1,0:T(8,128)(2,1)S(1)}, bf16[256,512]{1,0:T(8,128)(2,1)S(1)}, u32[]{:S(2)}, u32[]{:S(2)}) collective-permute-start(bf16[256,512]{1,0:T(8,128)(2,1)S(1)} %get-tuple-element.56), channel_id=1, source_target_pairs={{0,2},{1,3},{2,0},{3,1},{4,6},{5,7},{6,4},{7,5},{8,10},{9,11},{10,... | collective-permute-start | bytes 786440 | tf_op jit(solution)/shard_map/ppermute | solution.py:25
  78.2 1.9 %collective-permute-start.12 = (bf16[256,512]{1,0:T(8,128)(2,1)S(1)}, bf16[256,512]{1,0:T(8,128)(2,1)S(1)}, u32[]{:S(2)}, u32[]{:S(2)}) collective-permute-start(bf16[256,512]{1,0:T(8,128)(2,1)S(1)} %get-tuple-element.55), channel_id=1, source_target_pairs={{0,2},{1,3},{2,0},{3,1},{4,6},{5,7},{6,4},{7,5},{8,10},{9,11},{10,... | collective-permute-start | bytes 786440 | tf_op jit(solution)/shard_map/ppermute | solution.py:25
  80.1 3.5 %shard_map.90 = (bf16[256,1536]{1,0:T(8,128)(2,1)S(1)}, bf16[256,1536]{1,0:T(8,128)(2,1)S(1)}, f32[512,512]{1,0:T(8,128)S(1)}, f32[8,128]{1,0:T(8,128)}) custom-call(bf16[256,512]{1,0:T(8,128)(2,1)S(1)} %collective-permute-done.refs_0_, bf16[256,512]{1,0:T(8,128)(2,1)S(1)} %collective-permute-done.1.refs_1_, ...), custom_call_target="tpu_custom_call" | custom-call | flops 1572864 | bytes 7168 | tf_op jit(solution)/shard_map/pallas_call | solution.py:261
  84.2 1.6 %collective-permute-start.9 = (bf16[256,512]{1,0:T(8,128)(2,1)S(1)}, bf16[256,512]{1,0:T(8,128)(2,1)S(1)}, u32[]{:S(2)}, u32[]{:S(2)}) collective-permute-start(bf16[256,512]{1,0:T(8,128)(2,1)S(1)} %get-tuple-element.51), channel_id=1, source_target_pairs={{0,2},{1,3},{2,0},{3,1},{4,6},{5,7},{6,4},{7,5},{8,10},{9,11},{10,... | collective-permute-start | bytes 786440 | tf_op jit(solution)/shard_map/ppermute | solution.py:25
  86.6 3.1 %collective-permute-start.29 = (bf16[1024,128]{1,0:T(8,128)(2,1)S(1)}, bf16[1024,128]{1,0:T(8,128)(2,1)S(1)}, u32[]{:S(2)}, u32[]{:S(2)}) collective-permute-start(bf16[1024,128]{1,0:T(8,128)(2,1)S(1)} %get-tuple-element.83), channel_id=1, source_target_pairs={{0,28},{1,29},{2,30},{3,31},{4,0},{5,1},{6,2},{7,3},{8,4},{9,5},{1... | collective-permute-start | bytes 786440 | tf_op jit(solution)/shard_map/ppermute | solution.py:25
  89.7 2.6 %shard_map.91 = (bf16[256,1024]{1,0:T(8,128)(2,1)S(1)}, bf16[256,1024]{1,0:T(8,128)(2,1)S(1)}, f32[512,512]{1,0:T(8,128)S(1)}, f32[8,128]{1,0:T(8,128)}) custom-call(bf16[384,512]{1,0:T(8,128)(2,1)S(1)} %collective-permute-done.3.refs_0_.refs_4_, bf16[384,512]{1,0:T(8,128)(2,1)S(1)} %collective-permute-done.5.refs_1_.refs_5_, ...), custom_call_target="tpu_custom_call" | custom-call | flops 1048576 | bytes 6144 | tf_op jit(solution)/shard_map/pallas_call | solution.py:261
  92.3 2.1 %collective-permute-done.9.refs_2_ = bf16[256,512]{1,0:T(8,128)(2,1)S(1)} collective-permute-done((bf16[256,512]{1,0:T(8,128)(2,1)S(1)}, bf16[256,512]{1,0:T(8,128)(2,1)S(1)}, u32[]{:S(2)}, u32[]{:S(2)}) %collective-permute-start.9) | collective-permute-done | bytes 262176 | tf_op jit(solution)/shard_map/ppermute | solution.py:25
  94.4 1.7 %collective-permute-start.30 = (bf16[512,128]{1,0:T(8,128)(2,1)S(1)}, bf16[512,128]{1,0:T(8,128)(2,1)S(1)}, u32[]{:S(2)}, u32[]{:S(2)}) collective-permute-start(bf16[512,128]{1,0:T(8,128)(2,1)S(1)} %get-tuple-element.84), channel_id=1, source_target_pairs={{0,2},{1,3},{2,0},{3,1},{4,6},{5,7},{6,4},{7,5},{8,10},{9,11},{10,... | collective-permute-start | bytes 393224 | tf_op jit(solution)/shard_map/ppermute | solution.py:25
  96.1 2.6 %shard_map.92 = (bf16[256,1024]{1,0:T(8,128)(2,1)S(1)}, bf16[256,1024]{1,0:T(8,128)(2,1)S(1)}, f32[512,512]{1,0:T(8,128)S(1)}, f32[8,128]{1,0:T(8,128)}) custom-call(bf16[384,512]{1,0:T(8,128)(2,1)S(1)} %collective-permute-done.4.refs_0_.refs_3_, bf16[384,512]{1,0:T(8,128)(2,1)S(1)} %collective-permute-done.6.refs_1_.refs_4_, ...), custom_call_target="tpu_custom_call" | custom-call | flops 1048576 | bytes 6144 | tf_op jit(solution)/shard_map/pallas_call | solution.py:261
  98.6 1.2 shard_map.93
  99.8 1.2 collective-permute-done.30.yf
  102.3 5.8 %collective-permute-done.31.refs_0_ = bf16[256,512]{1,0:T(8,128)(2,1)S(1)} collective-permute-done((bf16[256,512]{1,0:T(8,128)(2,1)S(1)}, bf16[256,512]{1,0:T(8,128)(2,1)S(1)}, u32[]{:S(2)}, u32[]{:S(2)}) %collective-permute-start.31) | collective-permute-done | bytes 262176 | tf_op jit(solution)/shard_map/ppermute | solution.py:25
  108.1 0.7 collective-permute-start.36
  108.8 2.1 %collective-permute-start.35 = (bf16[256,512]{1,0:T(8,128)(2,1)S(1)}, bf16[256,512]{1,0:T(8,128)(2,1)S(1)}, u32[]{:S(2)}, u32[]{:S(2)}) collective-permute-start(bf16[256,512]{1,0:T(8,128)(2,1)S(1)} %get-tuple-element.87), channel_id=1, source_target_pairs={{0,64},{32,96},{64,0},{96,32},{128,192},{160,224},{192,128},{224,1... | collective-permute-start | bytes 786440 | tf_op jit(solution)/shard_map/ppermute | solution.py:25
  110.9 1.4 %collective-permute-start.34 = (bf16[256,512]{1,0:T(8,128)(2,1)S(1)}, bf16[256,512]{1,0:T(8,128)(2,1)S(1)}, u32[]{:S(2)}, u32[]{:S(2)}) collective-permute-start(bf16[256,512]{1,0:T(8,128)(2,1)S(1)} %get-tuple-element.87), channel_id=1, source_target_pairs={{0,32},{32,0},{64,96},{96,64},{128,160},{160,128},{192,224},{224,1... | collective-permute-start | bytes 786440 | tf_op jit(solution)/shard_map/ppermute | solution.py:25
  112.3 1.2 shard_map.103
  113.5 2.4 %shard_map.94.rest_0_ = bf16[256,8192]{1,0:T(8,128)(2,1)} custom-call(s32[11]{0:T(128)S(1)} %stack.47.where, bf16[256,1536]{1,0:T(8,128)(2,1)S(1)} %get-tuple-element.68.own, bf16[256,1536]{1,0:T(8,128)(2,1)S(1)} %collective-permute-done.18.sib), custom_call_target="tpu_custom_call" | custom-call | bytes 3072 | tf_op jit(solution)/shard_map/pallas_call | solution.py:306
  115.9 1.7 %shard_map.95.rest_0_ = bf16[256,8192]{1,0:T(8,128)(2,1)} custom-call(s32[11]{0:T(128)S(1)} %stack.47.where, bf16[256,1024]{1,0:T(8,128)(2,1)S(1)} %get-tuple-element.66.own, bf16[256,1024]{1,0:T(8,128)(2,1)S(1)} %collective-permute-done.17.sib, bf16[256,8192]{1,0:T(8,128)(2,1)} %shard_map.94.rest_0_), custom_call_target="tpu_custom_call", output_to_operand_aliasing={{}: (3, {})} | custom-call | bytes 2048 | tf_op jit(solution)/shard_map/pallas_call | solution.py:306
  117.6 1.7 %shard_map.96._ = bf16[256,8192]{1,0:T(8,128)(2,1)} custom-call(s32[11]{0:T(128)S(1)} %stack.47.where, bf16[256,1024]{1,0:T(8,128)(2,1)S(1)} %get-tuple-element.64.own, bf16[256,1024]{1,0:T(8,128)(2,1)S(1)} %collective-permute-done.16.sib, bf16[256,8192]{1,0:T(8,128)(2,1)} %shard_map.95.rest_0_), custom_call_target="tpu_custom_call", output_to_operand_aliasing={{}: (3, {})} | custom-call | bytes 2048 | tf_op jit(solution)/shard_map/pallas_call | solution.py:306
  119.3 1.5 %shard_map.97 = (bf16[256,8192]{1,0:T(8,128)(2,1)}, bf16[256,512]{1,0:T(8,128)(2,1)}) custom-call(s32[11]{0:T(128)S(1)} %stack.47.where, bf16[256,512]{1,0:T(8,128)(2,1)S(1)} %get-tuple-element.61.own, bf16[256,1024]{1,0:T(8,128)(2,1)S(1)} %collective-permute-done.15.sib, f32[256,512]{1,0:T(8,128)S(1)} %get-tuple-element.63.total, ...), custom_call_target="tpu_custom_call", output_to_operand_aliasing={{0}: (4, {})} | custom-call | bytes 1024 | tf_op jit(solution)/shard_map/pallas_call | solution.py:306
  120.8 1.0 collective-permute-done.34.rest_0_
  121.7 1.6 %shard_map.104 = (bf16[256,512]{1,0:T(8,128)(2,1)}, f32[256,512]{1,0:T(8,128)}) custom-call(s32[11]{0:T(128)S(1)} %stack.47.where, f32[1]{0:T(128)S(6)} %mul.8.rate, bf16[256,512]{1,0:T(8,128)(2,1)S(1)} %bitcast.34, f32[256,512]{1,0:T(8,128)S(1)} %get-tuple-element.85.moved, bf16[256,512]{1,0:T(8,128)(2,1)S(1)} %get-tuple-element.86.other_w, ...), custom_call_target="tpu_custom_call" | custom-call | bytes 3072 | tf_op jit(solution)/shard_map/pallas_call | solution.py:372
  (56 shorter events, 6.5 us)
Async XLA Ops:
  0.6 5.2 %copy-start = (bf16[1,256,512]{2,1,0:T(8,128)(2,1)S(1)}, bf16[1,256,512]{2,1,0:T(8,128)(2,1)}, u32[]{:S(2)}) copy-start(bf16[1,256,512]{2,1,0:T(8,128)(2,1)} %param.8) | copy-start | bytes 786436
  1.7 2.2 %copy-start.1 = (bf16[1,256,8192]{2,1,0:T(8,128)(2,1)S(1)}, bf16[1,256,8192]{2,1,0:T(8,128)(2,1)}, u32[]{:S(2)}) copy-start(bf16[1,256,8192]{2,1,0:T(8,128)(2,1)} %param.5) | copy-start | bytes 12582916
  3.8 2.5 %copy-start.2 = (bf16[1,256,512]{2,1,0:T(8,128)(2,1)S(1)}, bf16[1,256,512]{2,1,0:T(8,128)(2,1)}, u32[]{:S(2)}) copy-start(bf16[1,256,512]{2,1,0:T(8,128)(2,1)} %param.6) | copy-start | bytes 786436
  5.7 9.7 %collective-permute-start.10 = (bf16[256,4096]{1,0:T(8,128)(2,1)S(1)}, bf16[256,4096]{1,0:T(8,128)(2,1)S(1)}, u32[]{:S(2)}, u32[]{:S(2)}) collective-permute-start(bf16[256,4096]{1,0:T(8,128)(2,1)S(1)} %get-tuple-element.53), channel_id=1, source_target_pairs={{0,1},{1,0},{2,3},{3,2},{4,5},{5,4},{6,7},{7,6},{8,9},{9,8},{10,11... | collective-permute-start | bytes 6291464 | tf_op jit(solution)/shard_map/ppermute | solution.py:25
  5.8 9.5 %collective-permute-start.11 = (bf16[256,512]{1,0:T(8,128)(2,1)S(1)}, bf16[256,512]{1,0:T(8,128)(2,1)S(1)}, u32[]{:S(2)}, u32[]{:S(2)}) collective-permute-start(bf16[256,512]{1,0:T(8,128)(2,1)S(1)} %bitcast.20), channel_id=1, source_target_pairs={{0,1},{1,0},{2,3},{3,2},{4,5},{5,4},{6,7},{7,6},{8,9},{9,8},{10,11... | collective-permute-start | bytes 786440 | tf_op jit(solution)/shard_map/ppermute | solution.py:25
  6.3 17.2 %collective-permute-start.2 = (bf16[256,512]{1,0:T(8,128)(2,1)S(1)}, bf16[256,512]{1,0:T(8,128)(2,1)S(1)}, u32[]{:S(2)}, u32[]{:S(2)}) collective-permute-start(bf16[256,512]{1,0:T(8,128)(2,1)S(1)} %bitcast.27), channel_id=1, source_target_pairs={{0,2},{1,3},{2,0},{3,1},{4,6},{5,7},{6,4},{7,5},{8,10},{9,11},{10,... | collective-permute-start | bytes 786440 | tf_op jit(solution)/shard_map/ppermute | solution.py:25
  9.5 14.4 %collective-permute-start.1 = (bf16[256,512]{1,0:T(8,128)(2,1)S(1)}, bf16[256,512]{1,0:T(8,128)(2,1)S(1)}, u32[]{:S(2)}, u32[]{:S(2)}) collective-permute-start(bf16[256,512]{1,0:T(8,128)(2,1)S(1)} %bitcast.28), channel_id=1, source_target_pairs={{0,28},{1,29},{2,30},{3,31},{4,0},{5,1},{6,2},{7,3},{8,4},{9,5},{1... | collective-permute-start | bytes 786440 | tf_op jit(solution)/shard_map/ppermute | solution.py:25
  15.4 9.0 %collective-permute-start = (bf16[256,512]{1,0:T(8,128)(2,1)S(1)}, bf16[256,512]{1,0:T(8,128)(2,1)S(1)}, u32[]{:S(2)}, u32[]{:S(2)}) collective-permute-start(bf16[256,512]{1,0:T(8,128)(2,1)S(1)} %bitcast.29), channel_id=1, source_target_pairs={{0,4},{1,5},{2,6},{3,7},{4,8},{5,9},{6,10},{7,11},{8,12},{9,13},{1... | collective-permute-start | bytes 786440 | tf_op jit(solution)/shard_map/ppermute | solution.py:25
  19.9 10.8 %collective-permute-start.21 = (bf16[1024,128]{1,0:T(8,128)(2,1)S(1)}, bf16[1024,128]{1,0:T(8,128)(2,1)S(1)}, u32[]{:S(2)}, u32[]{:S(2)}) collective-permute-start(bf16[1024,128]{1,0:T(8,128)(2,1)S(1)} %get-tuple-element.75), channel_id=1, source_target_pairs={{0,2},{1,3},{2,0},{3,1},{4,6},{5,7},{6,4},{7,5},{8,10},{9,11},{10,... | collective-permute-start | bytes 786440 | tf_op jit(solution)/shard_map/ppermute | solution.py:25
  20.4 16.0 %collective-permute-start.20 = (bf16[1024,128]{1,0:T(8,128)(2,1)S(1)}, bf16[1024,128]{1,0:T(8,128)(2,1)S(1)}, u32[]{:S(2)}, u32[]{:S(2)}) collective-permute-start(bf16[1024,128]{1,0:T(8,128)(2,1)S(1)} %get-tuple-element.74), channel_id=1, source_target_pairs={{0,2},{1,3},{2,0},{3,1},{4,6},{5,7},{6,4},{7,5},{8,10},{9,11},{10,... | collective-permute-start | bytes 786440 | tf_op jit(solution)/shard_map/ppermute | solution.py:25
  23.6 27.5 %collective-permute-start.19 = (bf16[2560,128]{1,0:T(8,128)(2,1)S(1)}, bf16[2560,128]{1,0:T(8,128)(2,1)S(1)}, u32[]{:S(2)}, u32[]{:S(2)}) collective-permute-start(bf16[2560,128]{1,0:T(8,128)(2,1)S(1)} %get-tuple-element.73), channel_id=1, source_target_pairs={{0,2},{1,3},{2,0},{3,1},{4,6},{5,7},{6,4},{7,5},{8,10},{9,11},{10,... | collective-permute-start | bytes 1966088 | tf_op jit(solution)/shard_map/ppermute | solution.py:25
  25.0 22.8 %collective-permute-start.3 = (bf16[384,512]{1,0:T(8,128)(2,1)S(1)}, bf16[384,512]{1,0:T(8,128)(2,1)S(1)}, u32[]{:S(2)}, u32[]{:S(2)}) collective-permute-start(bf16[384,512]{1,0:T(8,128)(2,1)S(1)} %get-tuple-element.47), channel_id=1, source_target_pairs={{0,4},{1,5},{2,6},{3,7},{4,8},{5,9},{6,10},{7,11},{8,12},{9,13},{1... | collective-permute-start | bytes 1179656 | tf_op jit(solution)/shard_map/ppermute | solution.py:25
  25.0 22.8 %collective-permute-start.5 = (bf16[384,512]{1,0:T(8,128)(2,1)S(1)}, bf16[384,512]{1,0:T(8,128)(2,1)S(1)}, u32[]{:S(2)}, u32[]{:S(2)}) collective-permute-start(bf16[384,512]{1,0:T(8,128)(2,1)S(1)} %get-tuple-element.48), channel_id=1, source_target_pairs={{0,28},{1,29},{2,30},{3,31},{4,0},{5,1},{6,2},{7,3},{8,4},{9,5},{1... | collective-permute-start | bytes 1179656 | tf_op jit(solution)/shard_map/ppermute | solution.py:25
  31.4 11.0 %collective-permute-start.22 = (bf16[1024,128]{1,0:T(8,128)(2,1)S(1)}, bf16[1024,128]{1,0:T(8,128)(2,1)S(1)}, u32[]{:S(2)}, u32[]{:S(2)}) collective-permute-start(bf16[1024,128]{1,0:T(8,128)(2,1)S(1)} %get-tuple-element.76), channel_id=1, source_target_pairs={{0,4},{1,5},{2,6},{3,7},{4,8},{5,9},{6,10},{7,11},{8,12},{9,13},{1... | collective-permute-start | bytes 786440 | tf_op jit(solution)/shard_map/ppermute | solution.py:25
  36.4 7.1 %collective-permute-start.23 = (bf16[1024,128]{1,0:T(8,128)(2,1)S(1)}, bf16[1024,128]{1,0:T(8,128)(2,1)S(1)}, u32[]{:S(2)}, u32[]{:S(2)}) collective-permute-start(bf16[1024,128]{1,0:T(8,128)(2,1)S(1)} %get-tuple-element.77), channel_id=1, source_target_pairs={{0,28},{1,29},{2,30},{3,31},{4,0},{5,1},{6,2},{7,3},{8,4},{9,5},{1... | collective-permute-start | bytes 786440 | tf_op jit(solution)/shard_map/ppermute | solution.py:25
  44.2 13.7 %collective-permute-start.24 = (bf16[1536,128]{1,0:T(8,128)(2,1)S(1)}, bf16[1536,128]{1,0:T(8,128)(2,1)S(1)}, u32[]{:S(2)}, u32[]{:S(2)}) collective-permute-start(bf16[1536,128]{1,0:T(8,128)(2,1)S(1)} %get-tuple-element.78), channel_id=1, source_target_pairs={{0,4},{1,5},{2,6},{3,7},{4,8},{5,9},{6,10},{7,11},{8,12},{9,13},{1... | collective-permute-start | bytes 1179656 | tf_op jit(solution)/shard_map/ppermute | solution.py:25
  44.2 13.7 %collective-permute-start.25 = (bf16[1536,128]{1,0:T(8,128)(2,1)S(1)}, bf16[1536,128]{1,0:T(8,128)(2,1)S(1)}, u32[]{:S(2)}, u32[]{:S(2)}) collective-permute-start(bf16[1536,128]{1,0:T(8,128)(2,1)S(1)} %get-tuple-element.79), channel_id=1, source_target_pairs={{0,28},{1,29},{2,30},{3,31},{4,0},{5,1},{6,2},{7,3},{8,4},{9,5},{1... | collective-permute-start | bytes 1179656 | tf_op jit(solution)/shard_map/ppermute | solution.py:25
  47.9 18.5 %collective-permute-start.4 = (bf16[384,512]{1,0:T(8,128)(2,1)S(1)}, bf16[384,512]{1,0:T(8,128)(2,1)S(1)}, u32[]{:S(2)}, u32[]{:S(2)}) collective-permute-start(bf16[384,512]{1,0:T(8,128)(2,1)S(1)} %collective-permute-done.3.refs_0_.refs_4_), channel_id=1, source_target_pairs={{0,4},{1,5},{2,6},{3,7},{4,8},{5,9},{6,10},{7,11},{8,12},{9,13},{1... | collective-permute-start | bytes 1179656 | tf_op jit(solution)/shard_map/ppermute | solution.py:25
  47.9 20.5 %collective-permute-start.6 = (bf16[384,512]{1,0:T(8,128)(2,1)S(1)}, bf16[384,512]{1,0:T(8,128)(2,1)S(1)}, u32[]{:S(2)}, u32[]{:S(2)}) collective-permute-start(bf16[384,512]{1,0:T(8,128)(2,1)S(1)} %collective-permute-done.5.refs_1_.refs_5_), channel_id=1, source_target_pairs={{0,28},{1,29},{2,30},{3,31},{4,0},{5,1},{6,2},{7,3},{8,4},{9,5},{1... | collective-permute-start | bytes 1179656 | tf_op jit(solution)/shard_map/ppermute | solution.py:25
  51.1 17.9 %collective-permute-start.33 = (bf16[256,512]{1,0:T(8,128)(2,1)S(1)}, bf16[256,512]{1,0:T(8,128)(2,1)S(1)}, u32[]{:S(2)}, u32[]{:S(2)}) collective-permute-start(bf16[256,512]{1,0:T(8,128)(2,1)S(1)} %bitcast.30), channel_id=1, source_target_pairs={{0,128},{32,160},{64,192},{96,224},{128,0},{160,32},{192,64},{224,... | collective-permute-start | bytes 786440 | tf_op jit(solution)/shard_map/ppermute | solution.py:25
  58.6 25.0 %collective-permute-start.26 = (bf16[1536,128]{1,0:T(8,128)(2,1)S(1)}, bf16[1536,128]{1,0:T(8,128)(2,1)S(1)}, u32[]{:S(2)}, u32[]{:S(2)}) collective-permute-start(bf16[1536,128]{1,0:T(8,128)(2,1)S(1)} %get-tuple-element.80), channel_id=1, source_target_pairs={{0,4},{1,5},{2,6},{3,7},{4,8},{5,9},{6,10},{7,11},{8,12},{9,13},{1... | collective-permute-start | bytes 1179656 | tf_op jit(solution)/shard_map/ppermute | solution.py:25
  59.5 13.3 %collective-permute-start.14 = (bf16[256,512]{1,0:T(8,128)(2,1)S(1)}, bf16[256,512]{1,0:T(8,128)(2,1)S(1)}, u32[]{:S(2)}, u32[]{:S(2)}) collective-permute-start(bf16[256,512]{1,0:T(8,128)(2,1)S(1)} %get-tuple-element.57), channel_id=1, source_target_pairs={{0,2},{1,3},{2,0},{3,1},{4,6},{5,7},{6,4},{7,5},{8,10},{9,11},{10,... | collective-permute-start | bytes 786440 | tf_op jit(solution)/shard_map/ppermute | solution.py:25
  66.3 17.9 %collective-permute-start.27 = (bf16[1536,128]{1,0:T(8,128)(2,1)S(1)}, bf16[1536,128]{1,0:T(8,128)(2,1)S(1)}, u32[]{:S(2)}, u32[]{:S(2)}) collective-permute-start(bf16[1536,128]{1,0:T(8,128)(2,1)S(1)} %get-tuple-element.81), channel_id=1, source_target_pairs={{0,28},{1,29},{2,30},{3,31},{4,0},{5,1},{6,2},{7,3},{8,4},{9,5},{1... | collective-permute-start | bytes 1179656 | tf_op jit(solution)/shard_map/ppermute | solution.py:25
  69.0 7.6 %collective-permute-start.7 = (bf16[256,512]{1,0:T(8,128)(2,1)S(1)}, bf16[256,512]{1,0:T(8,128)(2,1)S(1)}, u32[]{:S(2)}, u32[]{:S(2)}) collective-permute-start(bf16[256,512]{1,0:T(8,128)(2,1)S(1)} %get-tuple-element.49), channel_id=1, source_target_pairs={{0,4},{1,5},{2,6},{3,7},{4,8},{5,9},{6,10},{7,11},{8,12},{9,13},{1... | collective-permute-start | bytes 786440 | tf_op jit(solution)/shard_map/ppermute | solution.py:25
  69.0 9.2 %collective-permute-start.8 = (bf16[256,512]{1,0:T(8,128)(2,1)S(1)}, bf16[256,512]{1,0:T(8,128)(2,1)S(1)}, u32[]{:S(2)}, u32[]{:S(2)}) collective-permute-start(bf16[256,512]{1,0:T(8,128)(2,1)S(1)} %get-tuple-element.50), channel_id=1, source_target_pairs={{0,28},{1,29},{2,30},{3,31},{4,0},{5,1},{6,2},{7,3},{8,4},{9,5},{1... | collective-permute-start | bytes 786440 | tf_op jit(solution)/shard_map/ppermute | solution.py:25
  72.8 13.6 %collective-permute-start.32 = (bf16[256,512]{1,0:T(8,128)(2,1)S(1)}, bf16[256,512]{1,0:T(8,128)(2,1)S(1)}, u32[]{:S(2)}, u32[]{:S(2)}) collective-permute-start(bf16[256,512]{1,0:T(8,128)(2,1)S(1)} %bitcast.31), channel_id=1, source_target_pairs={{0,64},{32,96},{64,0},{96,32},{128,192},{160,224},{192,128},{224,1... | collective-permute-start | bytes 786440 | tf_op jit(solution)/shard_map/ppermute | solution.py:25
  76.6 10.0 %collective-permute-start.13 = (bf16[256,512]{1,0:T(8,128)(2,1)S(1)}, bf16[256,512]{1,0:T(8,128)(2,1)S(1)}, u32[]{:S(2)}, u32[]{:S(2)}) collective-permute-start(bf16[256,512]{1,0:T(8,128)(2,1)S(1)} %get-tuple-element.56), channel_id=1, source_target_pairs={{0,2},{1,3},{2,0},{3,1},{4,6},{5,7},{6,4},{7,5},{8,10},{9,11},{10,... | collective-permute-start | bytes 786440 | tf_op jit(solution)/shard_map/ppermute | solution.py:25
  78.2 14.1 %collective-permute-start.12 = (bf16[256,512]{1,0:T(8,128)(2,1)S(1)}, bf16[256,512]{1,0:T(8,128)(2,1)S(1)}, u32[]{:S(2)}, u32[]{:S(2)}) collective-permute-start(bf16[256,512]{1,0:T(8,128)(2,1)S(1)} %get-tuple-element.55), channel_id=1, source_target_pairs={{0,2},{1,3},{2,0},{3,1},{4,6},{5,7},{6,4},{7,5},{8,10},{9,11},{10,... | collective-permute-start | bytes 786440 | tf_op jit(solution)/shard_map/ppermute | solution.py:25
  83.6 27.3 %collective-permute-start.18 = (bf16[256,1536]{1,0:T(8,128)(2,1)S(1)}, bf16[256,1536]{1,0:T(8,128)(2,1)S(1)}, u32[]{:S(2)}, u32[]{:S(2)}) collective-permute-start(bf16[256,1536]{1,0:T(8,128)(2,1)S(1)} %get-tuple-element.69), channel_id=1, source_target_pairs={{0,1},{1,0},{2,3},{3,2},{4,5},{5,4},{6,7},{7,6},{8,9},{9,8},{10,11... | collective-permute-start | bytes 2359304 | tf_op jit(solution)/shard_map/ppermute | solution.py:25
  84.2 10.2 %collective-permute-start.9 = (bf16[256,512]{1,0:T(8,128)(2,1)S(1)}, bf16[256,512]{1,0:T(8,128)(2,1)S(1)}, u32[]{:S(2)}, u32[]{:S(2)}) collective-permute-start(bf16[256,512]{1,0:T(8,128)(2,1)S(1)} %get-tuple-element.51), channel_id=1, source_target_pairs={{0,2},{1,3},{2,0},{3,1},{4,6},{5,7},{6,4},{7,5},{8,10},{9,11},{10,... | collective-permute-start | bytes 786440 | tf_op jit(solution)/shard_map/ppermute | solution.py:25
  86.4 15.1 %collective-permute-start.28 = (bf16[1024,128]{1,0:T(8,128)(2,1)S(1)}, bf16[1024,128]{1,0:T(8,128)(2,1)S(1)}, u32[]{:S(2)}, u32[]{:S(2)}) collective-permute-start(bf16[1024,128]{1,0:T(8,128)(2,1)S(1)} %get-tuple-element.82), channel_id=1, source_target_pairs={{0,4},{1,5},{2,6},{3,7},{4,8},{5,9},{6,10},{7,11},{8,12},{9,13},{1... | collective-permute-start | bytes 786440 | tf_op jit(solution)/shard_map/ppermute | solution.py:25
  86.6 15.0 %collective-permute-start.29 = (bf16[1024,128]{1,0:T(8,128)(2,1)S(1)}, bf16[1024,128]{1,0:T(8,128)(2,1)S(1)}, u32[]{:S(2)}, u32[]{:S(2)}) collective-permute-start(bf16[1024,128]{1,0:T(8,128)(2,1)S(1)} %get-tuple-element.83), channel_id=1, source_target_pairs={{0,28},{1,29},{2,30},{3,31},{4,0},{5,1},{6,2},{7,3},{8,4},{9,5},{1... | collective-permute-start | bytes 786440 | tf_op jit(solution)/shard_map/ppermute | solution.py:25
  92.2 16.5 %collective-permute-start.17 = (bf16[256,1024]{1,0:T(8,128)(2,1)S(1)}, bf16[256,1024]{1,0:T(8,128)(2,1)S(1)}, u32[]{:S(2)}, u32[]{:S(2)}) collective-permute-start(bf16[256,1024]{1,0:T(8,128)(2,1)S(1)} %get-tuple-element.67), channel_id=1, source_target_pairs={{0,1},{1,0},{2,3},{3,2},{4,5},{5,4},{6,7},{7,6},{8,9},{9,8},{10,11... | collective-permute-start | bytes 1572872 | tf_op jit(solution)/shard_map/ppermute | solution.py:25
  94.4 6.6 %collective-permute-start.30 = (bf16[512,128]{1,0:T(8,128)(2,1)S(1)}, bf16[512,128]{1,0:T(8,128)(2,1)S(1)}, u32[]{:S(2)}, u32[]{:S(2)}) collective-permute-start(bf16[512,128]{1,0:T(8,128)(2,1)S(1)} %get-tuple-element.84), channel_id=1, source_target_pairs={{0,2},{1,3},{2,0},{3,1},{4,6},{5,7},{6,4},{7,5},{8,10},{9,11},{10,... | collective-permute-start | bytes 393224 | tf_op jit(solution)/shard_map/ppermute | solution.py:25
  98.6 3.4 %copy-start.3 = (f32[1,256,512]{2,1,0:T(8,128)S(1)}, f32[1,256,512]{2,1,0:T(8,128)}, u32[]{:S(2)}) copy-start(f32[1,256,512]{2,1,0:T(8,128)} %param.7) | copy-start | bytes 1572868
  101.0 7.0 %collective-permute-start.31 = (bf16[256,512]{1,0:T(8,128)(2,1)S(1)}, bf16[256,512]{1,0:T(8,128)(2,1)S(1)}, u32[]{:S(2)}, u32[]{:S(2)}) collective-permute-start(bf16[256,512]{1,0:T(8,128)(2,1)S(1)} %bitcast.33), channel_id=1, source_target_pairs={{0,32},{32,0},{64,96},{96,64},{128,160},{160,128},{192,224},{224,1... | collective-permute-start | bytes 786440 | tf_op jit(solution)/shard_map/ppermute | solution.py:25
  101.6 16.0 %collective-permute-start.16 = (bf16[256,1024]{1,0:T(8,128)(2,1)S(1)}, bf16[256,1024]{1,0:T(8,128)(2,1)S(1)}, u32[]{:S(2)}, u32[]{:S(2)}) collective-permute-start(bf16[256,1024]{1,0:T(8,128)(2,1)S(1)} %get-tuple-element.65), channel_id=1, source_target_pairs={{0,1},{1,0},{2,3},{3,2},{4,5},{5,4},{6,7},{7,6},{8,9},{9,8},{10,11... | collective-permute-start | bytes 1572872 | tf_op jit(solution)/shard_map/ppermute | solution.py:25
  101.6 17.7 %collective-permute-start.15 = (bf16[256,1024]{1,0:T(8,128)(2,1)S(1)}, bf16[256,1024]{1,0:T(8,128)(2,1)S(1)}, u32[]{:S(2)}, u32[]{:S(2)}) collective-permute-start(bf16[256,1024]{1,0:T(8,128)(2,1)S(1)} %get-tuple-element.62), channel_id=1, source_target_pairs={{0,1},{1,0},{2,3},{3,2},{4,5},{5,4},{6,7},{7,6},{8,9},{9,8},{10,11... | collective-permute-start | bytes 1572872 | tf_op jit(solution)/shard_map/ppermute | solution.py:25
  108.1 12.7 %collective-permute-start.36 = (bf16[256,512]{1,0:T(8,128)(2,1)S(1)}, bf16[256,512]{1,0:T(8,128)(2,1)S(1)}, u32[]{:S(2)}, u32[]{:S(2)}) collective-permute-start(bf16[256,512]{1,0:T(8,128)(2,1)S(1)} %get-tuple-element.87), channel_id=1, source_target_pairs={{0,128},{32,160},{64,192},{96,224},{128,0},{160,32},{192,64},{224,... | collective-permute-start | bytes 786440 | tf_op jit(solution)/shard_map/ppermute | solution.py:25
  108.8 12.0 %collective-permute-start.35 = (bf16[256,512]{1,0:T(8,128)(2,1)S(1)}, bf16[256,512]{1,0:T(8,128)(2,1)S(1)}, u32[]{:S(2)}, u32[]{:S(2)}) collective-permute-start(bf16[256,512]{1,0:T(8,128)(2,1)S(1)} %get-tuple-element.87), channel_id=1, source_target_pairs={{0,64},{32,96},{64,0},{96,32},{128,192},{160,224},{192,128},{224,1... | collective-permute-start | bytes 786440 | tf_op jit(solution)/shard_map/ppermute | solution.py:25
  110.9 10.9 %collective-permute-start.34 = (bf16[256,512]{1,0:T(8,128)(2,1)S(1)}, bf16[256,512]{1,0:T(8,128)(2,1)S(1)}, u32[]{:S(2)}, u32[]{:S(2)}) collective-permute-start(bf16[256,512]{1,0:T(8,128)(2,1)S(1)} %get-tuple-element.87), channel_id=1, source_target_pairs={{0,32},{32,0},{64,96},{96,64},{128,160},{160,128},{192,224},{224,1... | collective-permute-start | bytes 786440 | tf_op jit(solution)/shard_map/ppermute | solution.py:25

commit v2 on v1

--- a/solution.py
+++ b/solution.py
@@ -78,7 +78,7 @@
         specs.append(pl.BlockSpec((rows, array.shape[1]), lambda i, index=index: (index, 0)))
         args.append(array)
     width = args[0].shape[1]
-    specs += [TOKEN] * len(after)
+    specs += [TOKEN if t.dtype == F32 else pl.BlockSpec((16, 128), lambda i: (0, 0)) for t in after]
     args += list(after)
     sizes = [sum(terms[0][2] for terms in segments) for segments in outs]
     shapes = [jax.ShapeDtypeStruct((rows, width), BF) for rows in sizes]
@@ -478,7 +478,8 @@
 
     pay_u, pay_d, t_s3 = combine(
         [loc(3), loc(4), loc(5), loc(6), (from_y2, KV, 0), (from_y2, KV, 1), su2, sd2],
-        [third(0, 4, 2, 6), third(1, 5, 3, 7)]
+        [third(0, 4, 2, 6), third(1, 5, 3, 7)],
+        after=(t_w,),
     )
     su3, sd3 = up(pay_u), down(pay_d)
 

time: 123 us -> 116 us (0.943)
  starting transfers between devices: 52 us -> 45.3 us
    ppermute x37, starting transfers between devices: 52 us -> 45.3 us  [send(): return lax.ppermute(value, axis, pairs)]
  transfers between devices with their start and end apart: 37 -> 37, of which waited for: 12 -> 15; matrix products, arithmetic and copies ran while one was open for 0% -> 0% of each run, Pallas kernels for 23% -> 24%
where the time goes in v2:
time: 116 us
  starting transfers between devices  45.3 us (39%)
  waiting for transfers between devices  35.5 us (31%)
  Pallas kernels  31 us (27%)
  local copies, waits for them, and re-layouts  2.29 us (2%)
  between operations  1.66 us (1%)
    ppermute x37, starting transfers between devices, send(): return lax.ppermute(value, axis, pairs)  45.3 us
    ppermute x37, waiting for transfers between devices, send(): return lax.ppermute(value, axis, pairs)  35.5 us
    pallas_call x4, Pallas kernels, products(): pl.pallas_call(partial(products_kernel, plan=plan, n_pieces=len(pieces),...  9.78 us
    pallas_call x4, Pallas kernels, place(): pl.pallas_call(kernel, grid_spec=pltpu.PrefetchScalarGridSpec(num_scalar_...  7.28 us
    pallas_call x8, Pallas kernels, combine(): pl.pallas_call(partial(combine_kernel, outs=outs), grid=(1,), in_specs=sp...  5.14 us
    pallas_call x1, Pallas kernels, partials(): pl.pallas_call(partial(partials_kernel, scale=scale), grid=(Z,), in_specs...  4.54 us
  transfers between devices with their start and end apart: 37, of which 15 were waited for; matrix products, arithmetic and copies ran while one was open for 0% of the time, Pallas kernels for 24%

profile of v2, /device:TPU:2, one launch (start us, length us, event | category | flops | bytes accessed | tf_op | source)
XLA Modules:
  0.0 115.7 jit_solution(15803773728858863442)
XLA Ops:
  1.7 2.2 %copy-done.1 = bf16[1,256,8192]{2,1,0:T(8,128)(2,1)S(1)} copy-done((bf16[1,256,8192]{2,1,0:T(8,128)(2,1)S(1)}, bf16[1,256,8192]{2,1,0:T(8,128)(2,1)}, u32[]{:S(2)}) %copy-start.1) | copy-done | bytes 4194328
  3.8 1.9 %shard_map.87 = (bf16[256,4096]{1,0:T(8,128)(2,1)S(1)}, bf16[256,4096]{1,0:T(8,128)(2,1)S(1)}) custom-call(s32[11]{0:T(128)S(1)} %stack.47.where, f32[1]{0:T(128)S(6)} %mul.8.rate, bf16[256,8192]{1,0:T(8,128)(2,1)S(1)} %bitcast.26), custom_call_target="tpu_custom_call" | custom-call | bytes 8192 | tf_op jit(solution)/shard_map/pallas_call | solution.py:135
  6.3 3.2 %collective-permute-start.2 = (bf16[256,512]{1,0:T(8,128)(2,1)S(1)}, bf16[256,512]{1,0:T(8,128)(2,1)S(1)}, u32[]{:S(2)}, u32[]{:S(2)}) collective-permute-start(bf16[256,512]{1,0:T(8,128)(2,1)S(1)} %bitcast.27), channel_id=1, source_target_pairs={{0,2},{1,3},{2,0},{3,1},{4,6},{5,7},{6,4},{7,5},{8,10},{9,11},{10,... | collective-permute-start | bytes 786440 | tf_op jit(solution)/shard_map/ppermute | solution.py:25
  9.5 5.9 %collective-permute-start.1 = (bf16[256,512]{1,0:T(8,128)(2,1)S(1)}, bf16[256,512]{1,0:T(8,128)(2,1)S(1)}, u32[]{:S(2)}, u32[]{:S(2)}) collective-permute-start(bf16[256,512]{1,0:T(8,128)(2,1)S(1)} %bitcast.28), channel_id=1, source_target_pairs={{0,28},{1,29},{2,30},{3,31},{4,0},{5,1},{6,2},{7,3},{8,4},{9,5},{1... | collective-permute-start | bytes 786440 | tf_op jit(solution)/shard_map/ppermute | solution.py:25
  15.4 4.5 %shard_map.88 = (bf16[1024,128]{1,0:T(8,128)(2,1)S(1)}, bf16[1024,128]{1,0:T(8,128)(2,1)S(1)}, bf16[2560,128]{1,0:T(8,128)(2,1)S(1)}, bf16[12288,128]{1,0:T(8,128)(2,1)S(1)}, f32[8,128]{1,0:T(8,128)S(1)}) custom-call(bf16[256,4096]{1,0:T(8,128)(2,1)S(1)} %get-tuple-element.53.mine.refs_7_.refs_5_.refs_3_, ...), custom_call_target="tpu_custom_call" | custom-call | flops 2097152 | bytes 9216 | tf_op jit(solution)/shard_map/pallas_call | solution.py:183
  20.9 3.4 %collective-permute-done.refs_0_ = bf16[256,512]{1,0:T(8,128)(2,1)S(1)} collective-permute-done((bf16[256,512]{1,0:T(8,128)(2,1)S(1)}, bf16[256,512]{1,0:T(8,128)(2,1)S(1)}, u32[]{:S(2)}, u32[]{:S(2)}) %collective-permute-start) | collective-permute-done | bytes 262176 | tf_op jit(solution)/shard_map/ppermute | solution.py:25
  24.3 0.7 shard_map.84
  25.0 3.2 %collective-permute-start.5 = (bf16[384,512]{1,0:T(8,128)(2,1)S(1)}, bf16[384,512]{1,0:T(8,128)(2,1)S(1)}, u32[]{:S(2)}, u32[]{:S(2)}) collective-permute-start(bf16[384,512]{1,0:T(8,128)(2,1)S(1)} %get-tuple-element.49), channel_id=1, source_target_pairs={{0,28},{1,29},{2,30},{3,31},{4,0},{5,1},{6,2},{7,3},{8,4},{9,5},{1... | collective-permute-start | bytes 1179656 | tf_op jit(solution)/shard_map/ppermute | solution.py:25
  28.6 0.7 collective-permute-done.21.refs_3_
  29.3 0.6 shard_map.98
  29.9 4.4 %collective-permute-start.23 = (bf16[1024,128]{1,0:T(8,128)(2,1)S(1)}, bf16[1024,128]{1,0:T(8,128)(2,1)S(1)}, u32[]{:S(2)}, u32[]{:S(2)}) collective-permute-start(bf16[1024,128]{1,0:T(8,128)(2,1)S(1)} %get-tuple-element.78), channel_id=1, source_target_pairs={{0,28},{1,29},{2,30},{3,31},{4,0},{5,1},{6,2},{7,3},{8,4},{9,5},{1... | collective-permute-start | bytes 786440 | tf_op jit(solution)/shard_map/ppermute | solution.py:25
  34.3 3.9 %collective-permute-done.3.refs_0_.refs_4_ = bf16[384,512]{1,0:T(8,128)(2,1)S(1)} collective-permute-done((bf16[384,512]{1,0:T(8,128)(2,1)S(1)}, bf16[384,512]{1,0:T(8,128)(2,1)S(1)}, u32[]{:S(2)}, u32[]{:S(2)}) %collective-permute-start.3) | collective-permute-done | bytes 393248 | tf_op jit(solution)/shard_map/ppermute | solution.py:25
  38.3 0.7 collective-permute-start.28
  39.0 2.1 %collective-permute-start.27 = (bf16[256,512]{1,0:T(8,128)(2,1)S(1)}, bf16[256,512]{1,0:T(8,128)(2,1)S(1)}, u32[]{:S(2)}, u32[]{:S(2)}) collective-permute-start(bf16[256,512]{1,0:T(8,128)(2,1)S(1)} %bitcast.31), channel_id=1, source_target_pairs={{0,64},{32,96},{64,0},{96,32},{128,192},{160,224},{192,128},{224,1... | collective-permute-start | bytes 786440 | tf_op jit(solution)/shard_map/ppermute | solution.py:25
  41.1 2.8 %collective-permute-done.22.refs_6_ = bf16[1024,128]{1,0:T(8,128)(2,1)S(1)} collective-permute-done((bf16[1024,128]{1,0:T(8,128)(2,1)S(1)}, bf16[1024,128]{1,0:T(8,128)(2,1)S(1)}, u32[]{:S(2)}, u32[]{:S(2)}) %collective-permute-start.22) | collective-permute-done | bytes 262176 | tf_op jit(solution)/shard_map/ppermute | solution.py:25
  43.9 2.3 %collective-permute-start.6 = (bf16[384,512]{1,0:T(8,128)(2,1)S(1)}, bf16[384,512]{1,0:T(8,128)(2,1)S(1)}, u32[]{:S(2)}, u32[]{:S(2)}) collective-permute-start(bf16[384,512]{1,0:T(8,128)(2,1)S(1)} %collective-permute-done.5.refs_1_.refs_5_), channel_id=1, source_target_pairs={{0,28},{1,29},{2,30},{3,31},{4,0},{5,1},{6,2},{7,3},{8,4},{9,5},{1... | collective-permute-start | bytes 1179656 | tf_op jit(solution)/shard_map/ppermute | solution.py:25
  46.2 0.6 shard_map.99
  47.5 3.3 %collective-permute-start.25 = (bf16[1536,128]{1,0:T(8,128)(2,1)S(1)}, bf16[1536,128]{1,0:T(8,128)(2,1)S(1)}, u32[]{:S(2)}, u32[]{:S(2)}) collective-permute-start(bf16[1536,128]{1,0:T(8,128)(2,1)S(1)} %get-tuple-element.80), channel_id=1, source_target_pairs={{0,28},{1,29},{2,30},{3,31},{4,0},{5,1},{6,2},{7,3},{8,4},{9,5},{1... | collective-permute-start | bytes 1179656 | tf_op jit(solution)/shard_map/ppermute | solution.py:25
  50.8 1.5 %collective-permute-done.4.refs_0_.refs_3_ = bf16[384,512]{1,0:T(8,128)(2,1)S(1)} collective-permute-done((bf16[384,512]{1,0:T(8,128)(2,1)S(1)}, bf16[384,512]{1,0:T(8,128)(2,1)S(1)}, u32[]{:S(2)}, u32[]{:S(2)}) %collective-permute-start.4) | collective-permute-done | bytes 393248 | tf_op jit(solution)/shard_map/ppermute | solution.py:25
  52.9 2.6 %collective-permute-done.6.refs_1_.refs_4_ = bf16[384,512]{1,0:T(8,128)(2,1)S(1)} collective-permute-done((bf16[384,512]{1,0:T(8,128)(2,1)S(1)}, bf16[384,512]{1,0:T(8,128)(2,1)S(1)}, u32[]{:S(2)}, u32[]{:S(2)}) %collective-permute-start.6) | collective-permute-done | bytes 393248 | tf_op jit(solution)/shard_map/ppermute | solution.py:25
  55.4 2.3 %collective-permute-start.14 = (bf16[256,512]{1,0:T(8,128)(2,1)S(1)}, bf16[256,512]{1,0:T(8,128)(2,1)S(1)}, u32[]{:S(2)}, u32[]{:S(2)}) collective-permute-start(bf16[256,512]{1,0:T(8,128)(2,1)S(1)} %get-tuple-element.58), channel_id=1, source_target_pairs={{0,2},{1,3},{2,0},{3,1},{4,6},{5,7},{6,4},{7,5},{8,10},{9,11},{10,... | collective-permute-start | bytes 786440 | tf_op jit(solution)/shard_map/ppermute | solution.py:25
  57.7 0.6 shard_map.85
  59.3 2.7 %collective-permute-done.19.refs_4_.refs_5_.refs_3_.from_y = bf16[2560,128]{1,0:T(8,128)(2,1)S(1)} collective-permute-done((bf16[2560,128]{1,0:T(8,128)(2,1)S(1)}, bf16[2560,128]{1,0:T(8,128)(2,1)S(1)}, u32[]{:S(2)}, u32[]{:S(2)}) %collective-permute-start.19) | collective-permute-done | bytes 655392 | tf_op jit(solution)/shard_map/ppermute | solution.py:25
  62.0 0.7 shard_map.101
  62.7 3.2 %collective-permute-start.8 = (bf16[256,512]{1,0:T(8,128)(2,1)S(1)}, bf16[256,512]{1,0:T(8,128)(2,1)S(1)}, u32[]{:S(2)}, u32[]{:S(2)}) collective-permute-start(bf16[256,512]{1,0:T(8,128)(2,1)S(1)} %get-tuple-element.51), channel_id=1, source_target_pairs={{0,28},{1,29},{2,30},{3,31},{4,0},{5,1},{6,2},{7,3},{8,4},{9,5},{1... | collective-permute-start | bytes 786440 | tf_op jit(solution)/shard_map/ppermute | solution.py:25
  66.6 2.2 %collective-permute-start.13 = (bf16[256,512]{1,0:T(8,128)(2,1)S(1)}, bf16[256,512]{1,0:T(8,128)(2,1)S(1)}, u32[]{:S(2)}, u32[]{:S(2)}) collective-permute-start(bf16[256,512]{1,0:T(8,128)(2,1)S(1)} %get-tuple-element.57), channel_id=1, source_target_pairs={{0,2},{1,3},{2,0},{3,1},{4,6},{5,7},{6,4},{7,5},{8,10},{9,11},{10,... | collective-permute-start | bytes 786440 | tf_op jit(solution)/shard_map/ppermute | solution.py:25
  68.8 3.5 %shard_map.90 = (bf16[256,1536]{1,0:T(8,128)(2,1)S(1)}, bf16[256,1536]{1,0:T(8,128)(2,1)S(1)}, f32[512,512]{1,0:T(8,128)S(1)}, f32[8,128]{1,0:T(8,128)}) custom-call(bf16[256,512]{1,0:T(8,128)(2,1)S(1)} %collective-permute-done.refs_0_, bf16[256,512]{1,0:T(8,128)(2,1)S(1)} %collective-permute-done.1.refs_1_, ...), custom_call_target="tpu_custom_call" | custom-call | flops 1572864 | bytes 7168 | tf_op jit(solution)/shard_map/pallas_call | solution.py:261
  72.3 1.4 %collective-permute-start.12 = (bf16[256,512]{1,0:T(8,128)(2,1)S(1)}, bf16[256,512]{1,0:T(8,128)(2,1)S(1)}, u32[]{:S(2)}, u32[]{:S(2)}) collective-permute-start(bf16[256,512]{1,0:T(8,128)(2,1)S(1)} %get-tuple-element.56), channel_id=1, source_target_pairs={{0,2},{1,3},{2,0},{3,1},{4,6},{5,7},{6,4},{7,5},{8,10},{9,11},{10,... | collective-permute-start | bytes 786440 | tf_op jit(solution)/shard_map/ppermute | solution.py:25
  74.3 2.2 %collective-permute-start.9 = (bf16[256,512]{1,0:T(8,128)(2,1)S(1)}, bf16[256,512]{1,0:T(8,128)(2,1)S(1)}, u32[]{:S(2)}, u32[]{:S(2)}) collective-permute-start(bf16[256,512]{1,0:T(8,128)(2,1)S(1)} %get-tuple-element.52), channel_id=1, source_target_pairs={{0,2},{1,3},{2,0},{3,1},{4,6},{5,7},{6,4},{7,5},{8,10},{9,11},{10,... | collective-permute-start | bytes 786440 | tf_op jit(solution)/shard_map/ppermute | solution.py:25
  76.5 0.6 shard_map.102
  77.2 1.0 collective-permute-start.31
  78.2 2.6 %shard_map.91 = (bf16[256,1024]{1,0:T(8,128)(2,1)S(1)}, bf16[256,1024]{1,0:T(8,128)(2,1)S(1)}, f32[512,512]{1,0:T(8,128)S(1)}, f32[8,128]{1,0:T(8,128)}) custom-call(bf16[384,512]{1,0:T(8,128)(2,1)S(1)} %collective-permute-done.3.refs_0_.refs_4_, bf16[384,512]{1,0:T(8,128)(2,1)S(1)} %collective-permute-done.5.refs_1_.refs_5_, ...), custom_call_target="tpu_custom_call" | custom-call | flops 1048576 | bytes 6144 | tf_op jit(solution)/shard_map/pallas_call | solution.py:261
  80.7 2.3 %collective-permute-done.12.refs_2_ = bf16[256,512]{1,0:T(8,128)(2,1)S(1)} collective-permute-done((bf16[256,512]{1,0:T(8,128)(2,1)S(1)}, bf16[256,512]{1,0:T(8,128)(2,1)S(1)}, u32[]{:S(2)}, u32[]{:S(2)}) %collective-permute-start.12) | collective-permute-done | bytes 262176 | tf_op jit(solution)/shard_map/ppermute | solution.py:25
  83.0 1.3 %collective-permute-start.33 = (bf16[512,128]{1,0:T(8,128)(2,1)S(1)}, bf16[512,128]{1,0:T(8,128)(2,1)S(1)}, u32[]{:S(2)}, u32[]{:S(2)}) collective-permute-start(bf16[512,128]{1,0:T(8,128)(2,1)S(1)} %get-tuple-element.86), channel_id=1, source_target_pairs={{0,2},{1,3},{2,0},{3,1},{4,6},{5,7},{6,4},{7,5},{8,10},{9,11},{10,... | collective-permute-start | bytes 393224 | tf_op jit(solution)/shard_map/ppermute | solution.py:25
  84.3 2.6 %shard_map.92 = (bf16[256,1024]{1,0:T(8,128)(2,1)S(1)}, bf16[256,1024]{1,0:T(8,128)(2,1)S(1)}, f32[512,512]{1,0:T(8,128)S(1)}, f32[8,128]{1,0:T(8,128)}) custom-call(bf16[384,512]{1,0:T(8,128)(2,1)S(1)} %collective-permute-done.4.refs_0_.refs_3_, bf16[384,512]{1,0:T(8,128)(2,1)S(1)} %collective-permute-done.6.refs_1_.refs_4_, ...), custom_call_target="tpu_custom_call" | custom-call | flops 1048576 | bytes 6144 | tf_op jit(solution)/shard_map/pallas_call | solution.py:261
  86.9 1.7 %collective-permute-done.9.refs_2_ = bf16[256,512]{1,0:T(8,128)(2,1)S(1)} collective-permute-done((bf16[256,512]{1,0:T(8,128)(2,1)S(1)}, bf16[256,512]{1,0:T(8,128)(2,1)S(1)}, u32[]{:S(2)}, u32[]{:S(2)}) %collective-permute-start.9) | collective-permute-done | bytes 262176 | tf_op jit(solution)/shard_map/ppermute | solution.py:25
  88.6 1.2 %shard_map.93 = (bf16[256,512]{1,0:T(8,128)(2,1)S(1)}, f32[256,512]{1,0:T(8,128)S(1)}, bf16[256,1024]{1,0:T(8,128)(2,1)S(1)}, f32[8,128]{1,0:T(8,128)}) custom-call(bf16[256,512]{1,0:T(8,128)(2,1)S(1)} %collective-permute-done.7.refs_0_.refs_3_, bf16[256,512]{1,0:T(8,128)(2,1)S(1)} %collective-permute-done.8.refs_1_.refs_4_, ...), custom_call_target="tpu_custom_call" | custom-call | flops 524288 | bytes 5120 | tf_op jit(solution)/shard_map/pallas_call | solution.py:261
  89.8 1.1 collective-permute-done.33.yf
  91.0 7.8 %collective-permute-done.32.sd = bf16[1024,128]{1,0:T(8,128)(2,1)S(1)} collective-permute-done((bf16[1024,128]{1,0:T(8,128)(2,1)S(1)}, bf16[1024,128]{1,0:T(8,128)(2,1)S(1)}, u32[]{:S(2)}, u32[]{:S(2)}) %collective-permute-start.32) | collective-permute-done | bytes 262176 | tf_op jit(solution)/shard_map/ppermute | solution.py:25
  99.0 1.0 collective-permute-start.36
  100.0 2.1 %collective-permute-start.35 = (bf16[256,512]{1,0:T(8,128)(2,1)S(1)}, bf16[256,512]{1,0:T(8,128)(2,1)S(1)}, u32[]{:S(2)}, u32[]{:S(2)}) collective-permute-start(bf16[256,512]{1,0:T(8,128)(2,1)S(1)} %get-tuple-element.89), channel_id=1, source_target_pairs={{0,64},{32,96},{64,0},{96,32},{128,192},{160,224},{192,128},{224,1... | collective-permute-start | bytes 786440 | tf_op jit(solution)/shard_map/ppermute | solution.py:25
  102.2 1.4 %collective-permute-start.34 = (bf16[256,512]{1,0:T(8,128)(2,1)S(1)}, bf16[256,512]{1,0:T(8,128)(2,1)S(1)}, u32[]{:S(2)}, u32[]{:S(2)}) collective-permute-start(bf16[256,512]{1,0:T(8,128)(2,1)S(1)} %get-tuple-element.89), channel_id=1, source_target_pairs={{0,32},{32,0},{64,96},{96,64},{128,160},{160,128},{192,224},{224,1... | collective-permute-start | bytes 786440 | tf_op jit(solution)/shard_map/ppermute | solution.py:25
  103.6 2.4 %shard_map.94.rest_0_ = bf16[256,8192]{1,0:T(8,128)(2,1)} custom-call(s32[11]{0:T(128)S(1)} %stack.47.where, bf16[256,1536]{1,0:T(8,128)(2,1)S(1)} %get-tuple-element.69.own, bf16[256,1536]{1,0:T(8,128)(2,1)S(1)} %collective-permute-done.18.sib), custom_call_target="tpu_custom_call" | custom-call | bytes 3072 | tf_op jit(solution)/shard_map/pallas_call | solution.py:306
  106.0 1.7 %shard_map.95.rest_0_ = bf16[256,8192]{1,0:T(8,128)(2,1)} custom-call(s32[11]{0:T(128)S(1)} %stack.47.where, bf16[256,1024]{1,0:T(8,128)(2,1)S(1)} %get-tuple-element.67.own, bf16[256,1024]{1,0:T(8,128)(2,1)S(1)} %collective-permute-done.17.sib, bf16[256,8192]{1,0:T(8,128)(2,1)} %shard_map.94.rest_0_), custom_call_target="tpu_custom_call", output_to_operand_aliasing={{}: (3, {})} | custom-call | bytes 2048 | tf_op jit(solution)/shard_map/pallas_call | solution.py:306
  107.7 1.7 %shard_map.96._ = bf16[256,8192]{1,0:T(8,128)(2,1)} custom-call(s32[11]{0:T(128)S(1)} %stack.47.where, bf16[256,1024]{1,0:T(8,128)(2,1)S(1)} %get-tuple-element.65.own, bf16[256,1024]{1,0:T(8,128)(2,1)S(1)} %collective-permute-done.16.sib, bf16[256,8192]{1,0:T(8,128)(2,1)} %shard_map.95.rest_0_), custom_call_target="tpu_custom_call", output_to_operand_aliasing={{}: (3, {})} | custom-call | bytes 2048 | tf_op jit(solution)/shard_map/pallas_call | solution.py:306
  109.4 1.5 %shard_map.97 = (bf16[256,8192]{1,0:T(8,128)(2,1)}, bf16[256,512]{1,0:T(8,128)(2,1)}) custom-call(s32[11]{0:T(128)S(1)} %stack.47.where, bf16[256,512]{1,0:T(8,128)(2,1)S(1)} %get-tuple-element.62.own, bf16[256,1024]{1,0:T(8,128)(2,1)S(1)} %collective-permute-done.15.sib, f32[256,512]{1,0:T(8,128)S(1)} %get-tuple-element.64.total, ...), custom_call_target="tpu_custom_call", output_to_operand_aliasing={{0}: (4, {})} | custom-call | bytes 1024 | tf_op jit(solution)/shard_map/pallas_call | solution.py:306
  110.9 3.2 %collective-permute-done.34.rest_0_ = bf16[256,512]{1,0:T(8,128)(2,1)S(1)} collective-permute-done((bf16[256,512]{1,0:T(8,128)(2,1)S(1)}, bf16[256,512]{1,0:T(8,128)(2,1)S(1)}, u32[]{:S(2)}, u32[]{:S(2)}) %collective-permute-start.34) | collective-permute-done | bytes 262176 | tf_op jit(solution)/shard_map/ppermute | solution.py:25
  114.1 1.5 %shard_map.104 = (bf16[256,512]{1,0:T(8,128)(2,1)}, f32[256,512]{1,0:T(8,128)}) custom-call(s32[11]{0:T(128)S(1)} %stack.47.where, f32[1]{0:T(128)S(6)} %mul.8.rate, bf16[256,512]{1,0:T(8,128)(2,1)S(1)} %bitcast.34, f32[256,512]{1,0:T(8,128)S(1)} %get-tuple-element.87.moved, bf16[256,512]{1,0:T(8,128)(2,1)S(1)} %get-tuple-element.88.other_w, ...), custom_call_target="tpu_custom_call" | custom-call | bytes 3072 | tf_op jit(solution)/shard_map/pallas_call | solution.py:372
  (56 shorter events, 5.7 us)
Async XLA Ops:
  0.6 5.2 %copy-start = (bf16[1,256,512]{2,1,0:T(8,128)(2,1)S(1)}, bf16[1,256,512]{2,1,0:T(8,128)(2,1)}, u32[]{:S(2)}) copy-start(bf16[1,256,512]{2,1,0:T(8,128)(2,1)} %param.8) | copy-start | bytes 786436
  1.7 2.2 %copy-start.1 = (bf16[1,256,8192]{2,1,0:T(8,128)(2,1)S(1)}, bf16[1,256,8192]{2,1,0:T(8,128)(2,1)}, u32[]{:S(2)}) copy-start(bf16[1,256,8192]{2,1,0:T(8,128)(2,1)} %param.5) | copy-start | bytes 12582916
  3.8 2.5 %copy-start.2 = (bf16[1,256,512]{2,1,0:T(8,128)(2,1)S(1)}, bf16[1,256,512]{2,1,0:T(8,128)(2,1)}, u32[]{:S(2)}) copy-start(bf16[1,256,512]{2,1,0:T(8,128)(2,1)} %param.6) | copy-start | bytes 786436
  5.7 9.7 %collective-permute-start.10 = (bf16[256,4096]{1,0:T(8,128)(2,1)S(1)}, bf16[256,4096]{1,0:T(8,128)(2,1)S(1)}, u32[]{:S(2)}, u32[]{:S(2)}) collective-permute-start(bf16[256,4096]{1,0:T(8,128)(2,1)S(1)} %get-tuple-element.54), channel_id=1, source_target_pairs={{0,1},{1,0},{2,3},{3,2},{4,5},{5,4},{6,7},{7,6},{8,9},{9,8},{10,11... | collective-permute-start | bytes 6291464 | tf_op jit(solution)/shard_map/ppermute | solution.py:25
  5.8 9.5 %collective-permute-start.11 = (bf16[256,512]{1,0:T(8,128)(2,1)S(1)}, bf16[256,512]{1,0:T(8,128)(2,1)S(1)}, u32[]{:S(2)}, u32[]{:S(2)}) collective-permute-start(bf16[256,512]{1,0:T(8,128)(2,1)S(1)} %bitcast.20), channel_id=1, source_target_pairs={{0,1},{1,0},{2,3},{3,2},{4,5},{5,4},{6,7},{7,6},{8,9},{9,8},{10,11... | collective-permute-start | bytes 786440 | tf_op jit(solution)/shard_map/ppermute | solution.py:25
  6.3 14.0 %collective-permute-start.2 = (bf16[256,512]{1,0:T(8,128)(2,1)S(1)}, bf16[256,512]{1,0:T(8,128)(2,1)S(1)}, u32[]{:S(2)}, u32[]{:S(2)}) collective-permute-start(bf16[256,512]{1,0:T(8,128)(2,1)S(1)} %bitcast.27), channel_id=1, source_target_pairs={{0,2},{1,3},{2,0},{3,1},{4,6},{5,7},{6,4},{7,5},{8,10},{9,11},{10,... | collective-permute-start | bytes 786440 | tf_op jit(solution)/shard_map/ppermute | solution.py:25
  9.5 11.4 %collective-permute-start.1 = (bf16[256,512]{1,0:T(8,128)(2,1)S(1)}, bf16[256,512]{1,0:T(8,128)(2,1)S(1)}, u32[]{:S(2)}, u32[]{:S(2)}) collective-permute-start(bf16[256,512]{1,0:T(8,128)(2,1)S(1)} %bitcast.28), channel_id=1, source_target_pairs={{0,28},{1,29},{2,30},{3,31},{4,0},{5,1},{6,2},{7,3},{8,4},{9,5},{1... | collective-permute-start | bytes 786440 | tf_op jit(solution)/shard_map/ppermute | solution.py:25
  15.4 9.0 %collective-permute-start = (bf16[256,512]{1,0:T(8,128)(2,1)S(1)}, bf16[256,512]{1,0:T(8,128)(2,1)S(1)}, u32[]{:S(2)}, u32[]{:S(2)}) collective-permute-start(bf16[256,512]{1,0:T(8,128)(2,1)S(1)} %bitcast.29), channel_id=1, source_target_pairs={{0,4},{1,5},{2,6},{3,7},{4,8},{5,9},{6,10},{7,11},{8,12},{9,13},{1... | collective-permute-start | bytes 786440 | tf_op jit(solution)/shard_map/ppermute | solution.py:25
  19.9 9.4 %collective-permute-start.21 = (bf16[1024,128]{1,0:T(8,128)(2,1)S(1)}, bf16[1024,128]{1,0:T(8,128)(2,1)S(1)}, u32[]{:S(2)}, u32[]{:S(2)}) collective-permute-start(bf16[1024,128]{1,0:T(8,128)(2,1)S(1)} %get-tuple-element.76), channel_id=1, source_target_pairs={{0,2},{1,3},{2,0},{3,1},{4,6},{5,7},{6,4},{7,5},{8,10},{9,11},{10,... | collective-permute-start | bytes 786440 | tf_op jit(solution)/shard_map/ppermute | solution.py:25
  25.0 13.3 %collective-permute-start.3 = (bf16[384,512]{1,0:T(8,128)(2,1)S(1)}, bf16[384,512]{1,0:T(8,128)(2,1)S(1)}, u32[]{:S(2)}, u32[]{:S(2)}) collective-permute-start(bf16[384,512]{1,0:T(8,128)(2,1)S(1)} %get-tuple-element.48), channel_id=1, source_target_pairs={{0,4},{1,5},{2,6},{3,7},{4,8},{5,9},{6,10},{7,11},{8,12},{9,13},{1... | collective-permute-start | bytes 1179656 | tf_op jit(solution)/shard_map/ppermute | solution.py:25
  25.0 13.3 %collective-permute-start.5 = (bf16[384,512]{1,0:T(8,128)(2,1)S(1)}, bf16[384,512]{1,0:T(8,128)(2,1)S(1)}, u32[]{:S(2)}, u32[]{:S(2)}) collective-permute-start(bf16[384,512]{1,0:T(8,128)(2,1)S(1)} %get-tuple-element.49), channel_id=1, source_target_pairs={{0,28},{1,29},{2,30},{3,31},{4,0},{5,1},{6,2},{7,3},{8,4},{9,5},{1... | collective-permute-start | bytes 1179656 | tf_op jit(solution)/shard_map/ppermute | solution.py:25
  28.2 10.7 %collective-permute-start.20 = (bf16[1024,128]{1,0:T(8,128)(2,1)S(1)}, bf16[1024,128]{1,0:T(8,128)(2,1)S(1)}, u32[]{:S(2)}, u32[]{:S(2)}) collective-permute-start(bf16[1024,128]{1,0:T(8,128)(2,1)S(1)} %get-tuple-element.75), channel_id=1, source_target_pairs={{0,2},{1,3},{2,0},{3,1},{4,6},{5,7},{6,4},{7,5},{8,10},{9,11},{10,... | collective-permute-start | bytes 786440 | tf_op jit(solution)/shard_map/ppermute | solution.py:25
  29.9 14.0 %collective-permute-start.22 = (bf16[1024,128]{1,0:T(8,128)(2,1)S(1)}, bf16[1024,128]{1,0:T(8,128)(2,1)S(1)}, u32[]{:S(2)}, u32[]{:S(2)}) collective-permute-start(bf16[1024,128]{1,0:T(8,128)(2,1)S(1)} %get-tuple-element.77), channel_id=1, source_target_pairs={{0,4},{1,5},{2,6},{3,7},{4,8},{5,9},{6,10},{7,11},{8,12},{9,13},{1... | collective-permute-start | bytes 786440 | tf_op jit(solution)/shard_map/ppermute | solution.py:25
  29.9 14.0 %collective-permute-start.23 = (bf16[1024,128]{1,0:T(8,128)(2,1)S(1)}, bf16[1024,128]{1,0:T(8,128)(2,1)S(1)}, u32[]{:S(2)}, u32[]{:S(2)}) collective-permute-start(bf16[1024,128]{1,0:T(8,128)(2,1)S(1)} %get-tuple-element.78), channel_id=1, source_target_pairs={{0,28},{1,29},{2,30},{3,31},{4,0},{5,1},{6,2},{7,3},{8,4},{9,5},{1... | collective-permute-start | bytes 786440 | tf_op jit(solution)/shard_map/ppermute | solution.py:25
  38.3 14.0 %collective-permute-start.4 = (bf16[384,512]{1,0:T(8,128)(2,1)S(1)}, bf16[384,512]{1,0:T(8,128)(2,1)S(1)}, u32[]{:S(2)}, u32[]{:S(2)}) collective-permute-start(bf16[384,512]{1,0:T(8,128)(2,1)S(1)} %collective-permute-done.3.refs_0_.refs_4_), channel_id=1, source_target_pairs={{0,4},{1,5},{2,6},{3,7},{4,8},{5,9},{6,10},{7,11},{8,12},{9,13},{1... | collective-permute-start | bytes 1179656 | tf_op jit(solution)/shard_map/ppermute | solution.py:25
  38.3 9.2 %collective-permute-start.28 = (bf16[256,512]{1,0:T(8,128)(2,1)S(1)}, bf16[256,512]{1,0:T(8,128)(2,1)S(1)}, u32[]{:S(2)}, u32[]{:S(2)}) collective-permute-start(bf16[256,512]{1,0:T(8,128)(2,1)S(1)} %bitcast.30), channel_id=1, source_target_pairs={{0,128},{32,160},{64,192},{96,224},{128,0},{160,32},{192,64},{224,... | collective-permute-start | bytes 786440 | tf_op jit(solution)/shard_map/ppermute | solution.py:25
  39.0 8.5 %collective-permute-start.27 = (bf16[256,512]{1,0:T(8,128)(2,1)S(1)}, bf16[256,512]{1,0:T(8,128)(2,1)S(1)}, u32[]{:S(2)}, u32[]{:S(2)}) collective-permute-start(bf16[256,512]{1,0:T(8,128)(2,1)S(1)} %bitcast.31), channel_id=1, source_target_pairs={{0,64},{32,96},{64,0},{96,32},{128,192},{160,224},{192,128},{224,1... | collective-permute-start | bytes 786440 | tf_op jit(solution)/shard_map/ppermute | solution.py:25
  43.9 18.1 %collective-permute-start.19 = (bf16[2560,128]{1,0:T(8,128)(2,1)S(1)}, bf16[2560,128]{1,0:T(8,128)(2,1)S(1)}, u32[]{:S(2)}, u32[]{:S(2)}) collective-permute-start(bf16[2560,128]{1,0:T(8,128)(2,1)S(1)} %get-tuple-element.74), channel_id=1, source_target_pairs={{0,2},{1,3},{2,0},{3,1},{4,6},{5,7},{6,4},{7,5},{8,10},{9,11},{10,... | collective-permute-start | bytes 1966088 | tf_op jit(solution)/shard_map/ppermute | solution.py:25
  43.9 11.5 %collective-permute-start.6 = (bf16[384,512]{1,0:T(8,128)(2,1)S(1)}, bf16[384,512]{1,0:T(8,128)(2,1)S(1)}, u32[]{:S(2)}, u32[]{:S(2)}) collective-permute-start(bf16[384,512]{1,0:T(8,128)(2,1)S(1)} %collective-permute-done.5.refs_1_.refs_5_), channel_id=1, source_target_pairs={{0,28},{1,29},{2,30},{3,31},{4,0},{5,1},{6,2},{7,3},{8,4},{9,5},{1... | collective-permute-start | bytes 1179656 | tf_op jit(solution)/shard_map/ppermute | solution.py:25
  47.5 14.6 %collective-permute-start.24 = (bf16[1536,128]{1,0:T(8,128)(2,1)S(1)}, bf16[1536,128]{1,0:T(8,128)(2,1)S(1)}, u32[]{:S(2)}, u32[]{:S(2)}) collective-permute-start(bf16[1536,128]{1,0:T(8,128)(2,1)S(1)} %get-tuple-element.79), channel_id=1, source_target_pairs={{0,4},{1,5},{2,6},{3,7},{4,8},{5,9},{6,10},{7,11},{8,12},{9,13},{1... | collective-permute-start | bytes 1179656 | tf_op jit(solution)/shard_map/ppermute | solution.py:25
  47.5 14.6 %collective-permute-start.25 = (bf16[1536,128]{1,0:T(8,128)(2,1)S(1)}, bf16[1536,128]{1,0:T(8,128)(2,1)S(1)}, u32[]{:S(2)}, u32[]{:S(2)}) collective-permute-start(bf16[1536,128]{1,0:T(8,128)(2,1)S(1)} %get-tuple-element.80), channel_id=1, source_target_pairs={{0,28},{1,29},{2,30},{3,31},{4,0},{5,1},{6,2},{7,3},{8,4},{9,5},{1... | collective-permute-start | bytes 1179656 | tf_op jit(solution)/shard_map/ppermute | solution.py:25
  52.3 6.4 %collective-permute-start.26 = (bf16[256,512]{1,0:T(8,128)(2,1)S(1)}, bf16[256,512]{1,0:T(8,128)(2,1)S(1)}, u32[]{:S(2)}, u32[]{:S(2)}) collective-permute-start(bf16[256,512]{1,0:T(8,128)(2,1)S(1)} %bitcast.32), channel_id=1, source_target_pairs={{0,32},{32,0},{64,96},{96,64},{128,160},{160,128},{192,224},{224,1... | collective-permute-start | bytes 786440 | tf_op jit(solution)/shard_map/ppermute | solution.py:25
  55.4 11.2 %collective-permute-start.14 = (bf16[256,512]{1,0:T(8,128)(2,1)S(1)}, bf16[256,512]{1,0:T(8,128)(2,1)S(1)}, u32[]{:S(2)}, u32[]{:S(2)}) collective-permute-start(bf16[256,512]{1,0:T(8,128)(2,1)S(1)} %get-tuple-element.58), channel_id=1, source_target_pairs={{0,2},{1,3},{2,0},{3,1},{4,6},{5,7},{6,4},{7,5},{8,10},{9,11},{10,... | collective-permute-start | bytes 786440 | tf_op jit(solution)/shard_map/ppermute | solution.py:25
  58.7 13.6 %collective-permute-start.7 = (bf16[256,512]{1,0:T(8,128)(2,1)S(1)}, bf16[256,512]{1,0:T(8,128)(2,1)S(1)}, u32[]{:S(2)}, u32[]{:S(2)}) collective-permute-start(bf16[256,512]{1,0:T(8,128)(2,1)S(1)} %get-tuple-element.50), channel_id=1, source_target_pairs={{0,4},{1,5},{2,6},{3,7},{4,8},{5,9},{6,10},{7,11},{8,12},{9,13},{1... | collective-permute-start | bytes 786440 | tf_op jit(solution)/shard_map/ppermute | solution.py:25
  62.7 11.6 %collective-permute-start.29 = (bf16[1536,128]{1,0:T(8,128)(2,1)S(1)}, bf16[1536,128]{1,0:T(8,128)(2,1)S(1)}, u32[]{:S(2)}, u32[]{:S(2)}) collective-permute-start(bf16[1536,128]{1,0:T(8,128)(2,1)S(1)} %get-tuple-element.82), channel_id=1, source_target_pairs={{0,4},{1,5},{2,6},{3,7},{4,8},{5,9},{6,10},{7,11},{8,12},{9,13},{1... | collective-permute-start | bytes 1179656 | tf_op jit(solution)/shard_map/ppermute | solution.py:25
  62.7 9.6 %collective-permute-start.8 = (bf16[256,512]{1,0:T(8,128)(2,1)S(1)}, bf16[256,512]{1,0:T(8,128)(2,1)S(1)}, u32[]{:S(2)}, u32[]{:S(2)}) collective-permute-start(bf16[256,512]{1,0:T(8,128)(2,1)S(1)} %get-tuple-element.51), channel_id=1, source_target_pairs={{0,28},{1,29},{2,30},{3,31},{4,0},{5,1},{6,2},{7,3},{8,4},{9,5},{1... | collective-permute-start | bytes 786440 | tf_op jit(solution)/shard_map/ppermute | solution.py:25
  66.0 10.6 %collective-permute-start.30 = (bf16[1536,128]{1,0:T(8,128)(2,1)S(1)}, bf16[1536,128]{1,0:T(8,128)(2,1)S(1)}, u32[]{:S(2)}, u32[]{:S(2)}) collective-permute-start(bf16[1536,128]{1,0:T(8,128)(2,1)S(1)} %get-tuple-element.83), channel_id=1, source_target_pairs={{0,28},{1,29},{2,30},{3,31},{4,0},{5,1},{6,2},{7,3},{8,4},{9,5},{1... | collective-permute-start | bytes 1179656 | tf_op jit(solution)/shard_map/ppermute | solution.py:25
  66.6 11.5 %collective-permute-start.13 = (bf16[256,512]{1,0:T(8,128)(2,1)S(1)}, bf16[256,512]{1,0:T(8,128)(2,1)S(1)}, u32[]{:S(2)}, u32[]{:S(2)}) collective-permute-start(bf16[256,512]{1,0:T(8,128)(2,1)S(1)} %get-tuple-element.57), channel_id=1, source_target_pairs={{0,2},{1,3},{2,0},{3,1},{4,6},{5,7},{6,4},{7,5},{8,10},{9,11},{10,... | collective-permute-start | bytes 786440 | tf_op jit(solution)/shard_map/ppermute | solution.py:25
  72.3 29.9 %collective-permute-start.18 = (bf16[256,1536]{1,0:T(8,128)(2,1)S(1)}, bf16[256,1536]{1,0:T(8,128)(2,1)S(1)}, u32[]{:S(2)}, u32[]{:S(2)}) collective-permute-start(bf16[256,1536]{1,0:T(8,128)(2,1)S(1)} %get-tuple-element.70), channel_id=1, source_target_pairs={{0,1},{1,0},{2,3},{3,2},{4,5},{5,4},{6,7},{7,6},{8,9},{9,8},{10,11... | collective-permute-start | bytes 2359304 | tf_op jit(solution)/shard_map/ppermute | solution.py:25
  72.3 10.7 %collective-permute-start.12 = (bf16[256,512]{1,0:T(8,128)(2,1)S(1)}, bf16[256,512]{1,0:T(8,128)(2,1)S(1)}, u32[]{:S(2)}, u32[]{:S(2)}) collective-permute-start(bf16[256,512]{1,0:T(8,128)(2,1)S(1)} %get-tuple-element.56), channel_id=1, source_target_pairs={{0,2},{1,3},{2,0},{3,1},{4,6},{5,7},{6,4},{7,5},{8,10},{9,11},{10,... | collective-permute-start | bytes 786440 | tf_op jit(solution)/shard_map/ppermute | solution.py:25
  74.3 14.3 %collective-permute-start.9 = (bf16[256,512]{1,0:T(8,128)(2,1)S(1)}, bf16[256,512]{1,0:T(8,128)(2,1)S(1)}, u32[]{:S(2)}, u32[]{:S(2)}) collective-permute-start(bf16[256,512]{1,0:T(8,128)(2,1)S(1)} %get-tuple-element.52), channel_id=1, source_target_pairs={{0,2},{1,3},{2,0},{3,1},{4,6},{5,7},{6,4},{7,5},{8,10},{9,11},{10,... | collective-permute-start | bytes 786440 | tf_op jit(solution)/shard_map/ppermute | solution.py:25
  77.2 13.8 %collective-permute-start.31 = (bf16[1024,128]{1,0:T(8,128)(2,1)S(1)}, bf16[1024,128]{1,0:T(8,128)(2,1)S(1)}, u32[]{:S(2)}, u32[]{:S(2)}) collective-permute-start(bf16[1024,128]{1,0:T(8,128)(2,1)S(1)} %get-tuple-element.84), channel_id=1, source_target_pairs={{0,4},{1,5},{2,6},{3,7},{4,8},{5,9},{6,10},{7,11},{8,12},{9,13},{1... | collective-permute-start | bytes 786440 | tf_op jit(solution)/shard_map/ppermute | solution.py:25
  80.7 19.3 %collective-permute-start.17 = (bf16[256,1024]{1,0:T(8,128)(2,1)S(1)}, bf16[256,1024]{1,0:T(8,128)(2,1)S(1)}, u32[]{:S(2)}, u32[]{:S(2)}) collective-permute-start(bf16[256,1024]{1,0:T(8,128)(2,1)S(1)} %get-tuple-element.68), channel_id=1, source_target_pairs={{0,1},{1,0},{2,3},{3,2},{4,5},{5,4},{6,7},{7,6},{8,9},{9,8},{10,11... | collective-permute-start | bytes 1572872 | tf_op jit(solution)/shard_map/ppermute | solution.py:25
  83.0 8.0 %collective-permute-start.33 = (bf16[512,128]{1,0:T(8,128)(2,1)S(1)}, bf16[512,128]{1,0:T(8,128)(2,1)S(1)}, u32[]{:S(2)}, u32[]{:S(2)}) collective-permute-start(bf16[512,128]{1,0:T(8,128)(2,1)S(1)} %get-tuple-element.86), channel_id=1, source_target_pairs={{0,2},{1,3},{2,0},{3,1},{4,6},{5,7},{6,4},{7,5},{8,10},{9,11},{10,... | collective-permute-start | bytes 393224 | tf_op jit(solution)/shard_map/ppermute | solution.py:25
  86.9 11.9 %copy-start.3 = (f32[1,256,512]{2,1,0:T(8,128)S(1)}, f32[1,256,512]{2,1,0:T(8,128)}, u32[]{:S(2)}) copy-start(f32[1,256,512]{2,1,0:T(8,128)} %param.7) | copy-start | bytes 1572868
  88.6 19.1 %collective-permute-start.16 = (bf16[256,1024]{1,0:T(8,128)(2,1)S(1)}, bf16[256,1024]{1,0:T(8,128)(2,1)S(1)}, u32[]{:S(2)}, u32[]{:S(2)}) collective-permute-start(bf16[256,1024]{1,0:T(8,128)(2,1)S(1)} %get-tuple-element.66), channel_id=1, source_target_pairs={{0,1},{1,0},{2,3},{3,2},{4,5},{5,4},{6,7},{7,6},{8,9},{9,8},{10,11... | collective-permute-start | bytes 1572872 | tf_op jit(solution)/shard_map/ppermute | solution.py:25
  91.0 7.9 %collective-permute-start.32 = (bf16[1024,128]{1,0:T(8,128)(2,1)S(1)}, bf16[1024,128]{1,0:T(8,128)(2,1)S(1)}, u32[]{:S(2)}, u32[]{:S(2)}) collective-permute-start(bf16[1024,128]{1,0:T(8,128)(2,1)S(1)} %get-tuple-element.85), channel_id=1, source_target_pairs={{0,28},{1,29},{2,30},{3,31},{4,0},{5,1},{6,2},{7,3},{8,4},{9,5},{1... | collective-permute-start | bytes 786440 | tf_op jit(solution)/shard_map/ppermute | solution.py:25
  91.0 18.4 %collective-permute-start.15 = (bf16[256,1024]{1,0:T(8,128)(2,1)S(1)}, bf16[256,1024]{1,0:T(8,128)(2,1)S(1)}, u32[]{:S(2)}, u32[]{:S(2)}) collective-permute-start(bf16[256,1024]{1,0:T(8,128)(2,1)S(1)} %get-tuple-element.63), channel_id=1, source_target_pairs={{0,1},{1,0},{2,3},{3,2},{4,5},{5,4},{6,7},{7,6},{8,9},{9,8},{10,11... | collective-permute-start | bytes 1572872 | tf_op jit(solution)/shard_map/ppermute | solution.py:25
  99.0 11.9 %collective-permute-start.36 = (bf16[256,512]{1,0:T(8,128)(2,1)S(1)}, bf16[256,512]{1,0:T(8,128)(2,1)S(1)}, u32[]{:S(2)}, u32[]{:S(2)}) collective-permute-start(bf16[256,512]{1,0:T(8,128)(2,1)S(1)} %get-tuple-element.89), channel_id=1, source_target_pairs={{0,128},{32,160},{64,192},{96,224},{128,0},{160,32},{192,64},{224,... | collective-permute-start | bytes 786440 | tf_op jit(solution)/shard_map/ppermute | solution.py:25
  100.0 10.9 %collective-permute-start.35 = (bf16[256,512]{1,0:T(8,128)(2,1)S(1)}, bf16[256,512]{1,0:T(8,128)(2,1)S(1)}, u32[]{:S(2)}, u32[]{:S(2)}) collective-permute-start(bf16[256,512]{1,0:T(8,128)(2,1)S(1)} %get-tuple-element.89), channel_id=1, source_target_pairs={{0,64},{32,96},{64,0},{96,32},{128,192},{160,224},{192,128},{224,1... | collective-permute-start | bytes 786440 | tf_op jit(solution)/shard_map/ppermute | solution.py:25
  102.2 12.0 %collective-permute-start.34 = (bf16[256,512]{1,0:T(8,128)(2,1)S(1)}, bf16[256,512]{1,0:T(8,128)(2,1)S(1)}, u32[]{:S(2)}, u32[]{:S(2)}) collective-permute-start(bf16[256,512]{1,0:T(8,128)(2,1)S(1)} %get-tuple-element.89), channel_id=1, source_target_pairs={{0,32},{32,0},{64,96},{96,64},{128,160},{160,128},{192,224},{224,1... | collective-permute-start | bytes 786440 | tf_op jit(solution)/shard_map/ppermute | solution.py:25

commit v3 on v2

--- a/solution.py
+++ b/solution.py
@@ -146,7 +146,7 @@
     )(where, rate, acts)
 
 
-def partials_kernel(mine, got, cot, got_cot, first, second, third, local, token, turned, *, scale):
+def partials_kernel(mine, got, cot, got_cot, first, second, third, local, token, turned, both, *, scale):
     step = pl.program_id(0)
     token[...] = jnp.zeros((8, 128), F32)
 
@@ -155,8 +155,9 @@
         turned[:, :SHARD] = cot[...].T
         turned[:, SHARD:] = got_cot[...].T
 
-    total = jnp.dot(turned[:, :SHARD], mine[...], preferred_element_type=F32)
-    total += jnp.dot(turned[:, SHARD:], got[...], preferred_element_type=F32)
+    both[:SHARD, :] = mine[...]
+    both[SHARD:, :] = got[...]
+    total = jnp.dot(turned[...], both[...], preferred_element_type=F32)
     total = (total * scale).astype(BF)
     own_a, own_b, other_a, other_b = (total[:, k * HALF : (k + 1) * HALF] for k in range(4))
     local[0:KV, :] = own_a
@@ -187,7 +188,7 @@
         out_specs=[pl.BlockSpec((rows, HALF), lambda i: (0, 0)) for rows in sizes]
         + [pl.BlockSpec((3 * KV, HALF), lambda i: (i, 0)), TOKEN],
         out_shape=[jax.ShapeDtypeStruct((rows, HALF), BF) for rows in sizes + (Z * 3 * KV,)] + [TOKEN_SHAPE],
-        scratch_shapes=[pltpu.VMEM((KV, 512), BF)],
+        scratch_shapes=[pltpu.VMEM((KV, 512), BF), pltpu.VMEM((512, 512), BF)],
         compiler_params=params(16),
         cost_estimate=cost(2 * 4096 * 512 * 512, 9 * MIB),
     )(mine, got, cot, got_cot)

time: 116 us -> 116 us (level)
  no operation moved by 1% of the time
where the time goes in v3:
time: 116 us
  starting transfers between devices  45.3 us (39%)
  waiting for transfers between devices  35.5 us (31%)
  Pallas kernels  31 us (27%)
  local copies, waits for them, and re-layouts  2.29 us (2%)
  between operations  1.66 us (1%)
    ppermute x37, starting transfers between devices, send(): return lax.ppermute(value, axis, pairs)  45.3 us
    ppermute x37, waiting for transfers between devices, send(): return lax.ppermute(value, axis, pairs)  35.5 us
    pallas_call x4, Pallas kernels, products(): pl.pallas_call(partial(products_kernel, plan=plan, n_pieces=len(pieces),...  9.78 us
    pallas_call x4, Pallas kernels, place(): pl.pallas_call(kernel, grid_spec=pltpu.PrefetchScalarGridSpec(num_scalar_...  7.28 us
    pallas_call x8, Pallas kernels, combine(): pl.pallas_call(partial(combine_kernel, outs=outs), grid=(1,), in_specs=sp...  5.14 us
    pallas_call x1, Pallas kernels, partials(): pl.pallas_call(partial(partials_kernel, scale=scale), grid=(Z,), in_specs...  4.54 us
  transfers between devices with their start and end apart: 37, of which 15 were waited for; matrix products, arithmetic and copies ran while one was open for 0% of the time, Pallas kernels for 24%

profile of v3, /device:TPU:2, one launch (start us, length us, event | category | flops | bytes accessed | tf_op | source)
XLA Modules:
  0.0 115.7 jit_solution(14665754265872152090)
XLA Ops:
  1.7 2.2 %copy-done.1 = bf16[1,256,8192]{2,1,0:T(8,128)(2,1)S(1)} copy-done((bf16[1,256,8192]{2,1,0:T(8,128)(2,1)S(1)}, bf16[1,256,8192]{2,1,0:T(8,128)(2,1)}, u32[]{:S(2)}) %copy-start.1) | copy-done | bytes 4194328
  3.8 1.9 %shard_map.87 = (bf16[256,4096]{1,0:T(8,128)(2,1)S(1)}, bf16[256,4096]{1,0:T(8,128)(2,1)S(1)}) custom-call(s32[11]{0:T(128)S(1)} %stack.47.where, f32[1]{0:T(128)S(6)} %mul.8.rate, bf16[256,8192]{1,0:T(8,128)(2,1)S(1)} %bitcast.26), custom_call_target="tpu_custom_call" | custom-call | bytes 8192 | tf_op jit(solution)/shard_map/pallas_call | solution.py:135
  6.3 3.2 %collective-permute-start.2 = (bf16[256,512]{1,0:T(8,128)(2,1)S(1)}, bf16[256,512]{1,0:T(8,128)(2,1)S(1)}, u32[]{:S(2)}, u32[]{:S(2)}) collective-permute-start(bf16[256,512]{1,0:T(8,128)(2,1)S(1)} %bitcast.27), channel_id=1, source_target_pairs={{0,2},{1,3},{2,0},{3,1},{4,6},{5,7},{6,4},{7,5},{8,10},{9,11},{10,... | collective-permute-start | bytes 786440 | tf_op jit(solution)/shard_map/ppermute | solution.py:25
  9.5 5.9 %collective-permute-start.1 = (bf16[256,512]{1,0:T(8,128)(2,1)S(1)}, bf16[256,512]{1,0:T(8,128)(2,1)S(1)}, u32[]{:S(2)}, u32[]{:S(2)}) collective-permute-start(bf16[256,512]{1,0:T(8,128)(2,1)S(1)} %bitcast.28), channel_id=1, source_target_pairs={{0,28},{1,29},{2,30},{3,31},{4,0},{5,1},{6,2},{7,3},{8,4},{9,5},{1... | collective-permute-start | bytes 786440 | tf_op jit(solution)/shard_map/ppermute | solution.py:25
  15.4 4.5 %shard_map.88 = (bf16[1024,128]{1,0:T(8,128)(2,1)S(1)}, bf16[1024,128]{1,0:T(8,128)(2,1)S(1)}, bf16[2560,128]{1,0:T(8,128)(2,1)S(1)}, bf16[12288,128]{1,0:T(8,128)(2,1)S(1)}, f32[8,128]{1,0:T(8,128)S(1)}) custom-call(bf16[256,4096]{1,0:T(8,128)(2,1)S(1)} %get-tuple-element.53.mine.refs_7_.refs_5_.refs_3_, ...), custom_call_target="tpu_custom_call" | custom-call | flops 2097152 | bytes 9216 | tf_op jit(solution)/shard_map/pallas_call | solution.py:184
  20.9 3.4 %collective-permute-done.refs_0_ = bf16[256,512]{1,0:T(8,128)(2,1)S(1)} collective-permute-done((bf16[256,512]{1,0:T(8,128)(2,1)S(1)}, bf16[256,512]{1,0:T(8,128)(2,1)S(1)}, u32[]{:S(2)}, u32[]{:S(2)}) %collective-permute-start) | collective-permute-done | bytes 262176 | tf_op jit(solution)/shard_map/ppermute | solution.py:25
  24.3 0.7 shard_map.84
  25.0 3.2 %collective-permute-start.5 = (bf16[384,512]{1,0:T(8,128)(2,1)S(1)}, bf16[384,512]{1,0:T(8,128)(2,1)S(1)}, u32[]{:S(2)}, u32[]{:S(2)}) collective-permute-start(bf16[384,512]{1,0:T(8,128)(2,1)S(1)} %get-tuple-element.49), channel_id=1, source_target_pairs={{0,28},{1,29},{2,30},{3,31},{4,0},{5,1},{6,2},{7,3},{8,4},{9,5},{1... | collective-permute-start | bytes 1179656 | tf_op jit(solution)/shard_map/ppermute | solution.py:25
  28.6 0.7 collective-permute-done.21.refs_3_
  29.3 0.6 shard_map.98
  29.9 4.4 %collective-permute-start.23 = (bf16[1024,128]{1,0:T(8,128)(2,1)S(1)}, bf16[1024,128]{1,0:T(8,128)(2,1)S(1)}, u32[]{:S(2)}, u32[]{:S(2)}) collective-permute-start(bf16[1024,128]{1,0:T(8,128)(2,1)S(1)} %get-tuple-element.78), channel_id=1, source_target_pairs={{0,28},{1,29},{2,30},{3,31},{4,0},{5,1},{6,2},{7,3},{8,4},{9,5},{1... | collective-permute-start | bytes 786440 | tf_op jit(solution)/shard_map/ppermute | solution.py:25
  34.3 3.9 %collective-permute-done.3.refs_0_.refs_4_ = bf16[384,512]{1,0:T(8,128)(2,1)S(1)} collective-permute-done((bf16[384,512]{1,0:T(8,128)(2,1)S(1)}, bf16[384,512]{1,0:T(8,128)(2,1)S(1)}, u32[]{:S(2)}, u32[]{:S(2)}) %collective-permute-start.3) | collective-permute-done | bytes 393248 | tf_op jit(solution)/shard_map/ppermute | solution.py:25
  38.3 0.7 collective-permute-start.28
  39.0 2.1 %collective-permute-start.27 = (bf16[256,512]{1,0:T(8,128)(2,1)S(1)}, bf16[256,512]{1,0:T(8,128)(2,1)S(1)}, u32[]{:S(2)}, u32[]{:S(2)}) collective-permute-start(bf16[256,512]{1,0:T(8,128)(2,1)S(1)} %bitcast.31), channel_id=1, source_target_pairs={{0,64},{32,96},{64,0},{96,32},{128,192},{160,224},{192,128},{224,1... | collective-permute-start | bytes 786440 | tf_op jit(solution)/shard_map/ppermute | solution.py:25
  41.1 2.8 %collective-permute-done.22.refs_6_ = bf16[1024,128]{1,0:T(8,128)(2,1)S(1)} collective-permute-done((bf16[1024,128]{1,0:T(8,128)(2,1)S(1)}, bf16[1024,128]{1,0:T(8,128)(2,1)S(1)}, u32[]{:S(2)}, u32[]{:S(2)}) %collective-permute-start.22) | collective-permute-done | bytes 262176 | tf_op jit(solution)/shard_map/ppermute | solution.py:25
  43.9 2.3 %collective-permute-start.6 = (bf16[384,512]{1,0:T(8,128)(2,1)S(1)}, bf16[384,512]{1,0:T(8,128)(2,1)S(1)}, u32[]{:S(2)}, u32[]{:S(2)}) collective-permute-start(bf16[384,512]{1,0:T(8,128)(2,1)S(1)} %collective-permute-done.5.refs_1_.refs_5_), channel_id=1, source_target_pairs={{0,28},{1,29},{2,30},{3,31},{4,0},{5,1},{6,2},{7,3},{8,4},{9,5},{1... | collective-permute-start | bytes 1179656 | tf_op jit(solution)/shard_map/ppermute | solution.py:25
  46.2 0.6 shard_map.99
  47.5 3.3 %collective-permute-start.25 = (bf16[1536,128]{1,0:T(8,128)(2,1)S(1)}, bf16[1536,128]{1,0:T(8,128)(2,1)S(1)}, u32[]{:S(2)}, u32[]{:S(2)}) collective-permute-start(bf16[1536,128]{1,0:T(8,128)(2,1)S(1)} %get-tuple-element.80), channel_id=1, source_target_pairs={{0,28},{1,29},{2,30},{3,31},{4,0},{5,1},{6,2},{7,3},{8,4},{9,5},{1... | collective-permute-start | bytes 1179656 | tf_op jit(solution)/shard_map/ppermute | solution.py:25
  50.8 1.5 %collective-permute-done.4.refs_0_.refs_3_ = bf16[384,512]{1,0:T(8,128)(2,1)S(1)} collective-permute-done((bf16[384,512]{1,0:T(8,128)(2,1)S(1)}, bf16[384,512]{1,0:T(8,128)(2,1)S(1)}, u32[]{:S(2)}, u32[]{:S(2)}) %collective-permute-start.4) | collective-permute-done | bytes 393248 | tf_op jit(solution)/shard_map/ppermute | solution.py:25
  52.9 2.6 %collective-permute-done.6.refs_1_.refs_4_ = bf16[384,512]{1,0:T(8,128)(2,1)S(1)} collective-permute-done((bf16[384,512]{1,0:T(8,128)(2,1)S(1)}, bf16[384,512]{1,0:T(8,128)(2,1)S(1)}, u32[]{:S(2)}, u32[]{:S(2)}) %collective-permute-start.6) | collective-permute-done | bytes 393248 | tf_op jit(solution)/shard_map/ppermute | solution.py:25
  55.4 2.3 %collective-permute-start.14 = (bf16[256,512]{1,0:T(8,128)(2,1)S(1)}, bf16[256,512]{1,0:T(8,128)(2,1)S(1)}, u32[]{:S(2)}, u32[]{:S(2)}) collective-permute-start(bf16[256,512]{1,0:T(8,128)(2,1)S(1)} %get-tuple-element.58), channel_id=1, source_target_pairs={{0,2},{1,3},{2,0},{3,1},{4,6},{5,7},{6,4},{7,5},{8,10},{9,11},{10,... | collective-permute-start | bytes 786440 | tf_op jit(solution)/shard_map/ppermute | solution.py:25
  57.7 0.6 shard_map.85
  59.3 2.7 %collective-permute-done.19.refs_4_.refs_5_.refs_3_.from_y = bf16[2560,128]{1,0:T(8,128)(2,1)S(1)} collective-permute-done((bf16[2560,128]{1,0:T(8,128)(2,1)S(1)}, bf16[2560,128]{1,0:T(8,128)(2,1)S(1)}, u32[]{:S(2)}, u32[]{:S(2)}) %collective-permute-start.19) | collective-permute-done | bytes 655392 | tf_op jit(solution)/shard_map/ppermute | solution.py:25
  62.0 0.7 shard_map.101
  62.7 3.2 %collective-permute-start.8 = (bf16[256,512]{1,0:T(8,128)(2,1)S(1)}, bf16[256,512]{1,0:T(8,128)(2,1)S(1)}, u32[]{:S(2)}, u32[]{:S(2)}) collective-permute-start(bf16[256,512]{1,0:T(8,128)(2,1)S(1)} %get-tuple-element.51), channel_id=1, source_target_pairs={{0,28},{1,29},{2,30},{3,31},{4,0},{5,1},{6,2},{7,3},{8,4},{9,5},{1... | collective-permute-start | bytes 786440 | tf_op jit(solution)/shard_map/ppermute | solution.py:25
  66.6 2.2 %collective-permute-start.13 = (bf16[256,512]{1,0:T(8,128)(2,1)S(1)}, bf16[256,512]{1,0:T(8,128)(2,1)S(1)}, u32[]{:S(2)}, u32[]{:S(2)}) collective-permute-start(bf16[256,512]{1,0:T(8,128)(2,1)S(1)} %get-tuple-element.57), channel_id=1, source_target_pairs={{0,2},{1,3},{2,0},{3,1},{4,6},{5,7},{6,4},{7,5},{8,10},{9,11},{10,... | collective-permute-start | bytes 786440 | tf_op jit(solution)/shard_map/ppermute | solution.py:25
  68.8 3.5 %shard_map.90 = (bf16[256,1536]{1,0:T(8,128)(2,1)S(1)}, bf16[256,1536]{1,0:T(8,128)(2,1)S(1)}, f32[512,512]{1,0:T(8,128)S(1)}, f32[8,128]{1,0:T(8,128)}) custom-call(bf16[256,512]{1,0:T(8,128)(2,1)S(1)} %collective-permute-done.refs_0_, bf16[256,512]{1,0:T(8,128)(2,1)S(1)} %collective-permute-done.1.refs_1_, ...), custom_call_target="tpu_custom_call" | custom-call | flops 1572864 | bytes 7168 | tf_op jit(solution)/shard_map/pallas_call | solution.py:262
  72.3 1.4 %collective-permute-start.12 = (bf16[256,512]{1,0:T(8,128)(2,1)S(1)}, bf16[256,512]{1,0:T(8,128)(2,1)S(1)}, u32[]{:S(2)}, u32[]{:S(2)}) collective-permute-start(bf16[256,512]{1,0:T(8,128)(2,1)S(1)} %get-tuple-element.56), channel_id=1, source_target_pairs={{0,2},{1,3},{2,0},{3,1},{4,6},{5,7},{6,4},{7,5},{8,10},{9,11},{10,... | collective-permute-start | bytes 786440 | tf_op jit(solution)/shard_map/ppermute | solution.py:25
  74.3 2.2 %collective-permute-start.9 = (bf16[256,512]{1,0:T(8,128)(2,1)S(1)}, bf16[256,512]{1,0:T(8,128)(2,1)S(1)}, u32[]{:S(2)}, u32[]{:S(2)}) collective-permute-start(bf16[256,512]{1,0:T(8,128)(2,1)S(1)} %get-tuple-element.52), channel_id=1, source_target_pairs={{0,2},{1,3},{2,0},{3,1},{4,6},{5,7},{6,4},{7,5},{8,10},{9,11},{10,... | collective-permute-start | bytes 786440 | tf_op jit(solution)/shard_map/ppermute | solution.py:25
  76.5 0.6 shard_map.102
  77.2 1.0 collective-permute-start.31
  78.2 2.6 %shard_map.91 = (bf16[256,1024]{1,0:T(8,128)(2,1)S(1)}, bf16[256,1024]{1,0:T(8,128)(2,1)S(1)}, f32[512,512]{1,0:T(8,128)S(1)}, f32[8,128]{1,0:T(8,128)}) custom-call(bf16[384,512]{1,0:T(8,128)(2,1)S(1)} %collective-permute-done.3.refs_0_.refs_4_, bf16[384,512]{1,0:T(8,128)(2,1)S(1)} %collective-permute-done.5.refs_1_.refs_5_, ...), custom_call_target="tpu_custom_call" | custom-call | flops 1048576 | bytes 6144 | tf_op jit(solution)/shard_map/pallas_call | solution.py:262
  80.7 2.3 %collective-permute-done.12.refs_2_ = bf16[256,512]{1,0:T(8,128)(2,1)S(1)} collective-permute-done((bf16[256,512]{1,0:T(8,128)(2,1)S(1)}, bf16[256,512]{1,0:T(8,128)(2,1)S(1)}, u32[]{:S(2)}, u32[]{:S(2)}) %collective-permute-start.12) | collective-permute-done | bytes 262176 | tf_op jit(solution)/shard_map/ppermute | solution.py:25
  83.0 1.3 %collective-permute-start.33 = (bf16[512,128]{1,0:T(8,128)(2,1)S(1)}, bf16[512,128]{1,0:T(8,128)(2,1)S(1)}, u32[]{:S(2)}, u32[]{:S(2)}) collective-permute-start(bf16[512,128]{1,0:T(8,128)(2,1)S(1)} %get-tuple-element.86), channel_id=1, source_target_pairs={{0,2},{1,3},{2,0},{3,1},{4,6},{5,7},{6,4},{7,5},{8,10},{9,11},{10,... | collective-permute-start | bytes 393224 | tf_op jit(solution)/shard_map/ppermute | solution.py:25
  84.3 2.6 %shard_map.92 = (bf16[256,1024]{1,0:T(8,128)(2,1)S(1)}, bf16[256,1024]{1,0:T(8,128)(2,1)S(1)}, f32[512,512]{1,0:T(8,128)S(1)}, f32[8,128]{1,0:T(8,128)}) custom-call(bf16[384,512]{1,0:T(8,128)(2,1)S(1)} %collective-permute-done.4.refs_0_.refs_3_, bf16[384,512]{1,0:T(8,128)(2,1)S(1)} %collective-permute-done.6.refs_1_.refs_4_, ...), custom_call_target="tpu_custom_call" | custom-call | flops 1048576 | bytes 6144 | tf_op jit(solution)/shard_map/pallas_call | solution.py:262
  86.9 1.7 %collective-permute-done.9.refs_2_ = bf16[256,512]{1,0:T(8,128)(2,1)S(1)} collective-permute-done((bf16[256,512]{1,0:T(8,128)(2,1)S(1)}, bf16[256,512]{1,0:T(8,128)(2,1)S(1)}, u32[]{:S(2)}, u32[]{:S(2)}) %collective-permute-start.9) | collective-permute-done | bytes 262176 | tf_op jit(solution)/shard_map/ppermute | solution.py:25
  88.6 1.2 %shard_map.93 = (bf16[256,512]{1,0:T(8,128)(2,1)S(1)}, f32[256,512]{1,0:T(8,128)S(1)}, bf16[256,1024]{1,0:T(8,128)(2,1)S(1)}, f32[8,128]{1,0:T(8,128)}) custom-call(bf16[256,512]{1,0:T(8,128)(2,1)S(1)} %collective-permute-done.7.refs_0_.refs_3_, bf16[256,512]{1,0:T(8,128)(2,1)S(1)} %collective-permute-done.8.refs_1_.refs_4_, ...), custom_call_target="tpu_custom_call" | custom-call | flops 524288 | bytes 5120 | tf_op jit(solution)/shard_map/pallas_call | solution.py:262
  89.8 1.1 collective-permute-done.33.yf
  91.0 7.8 %collective-permute-done.32.sd = bf16[1024,128]{1,0:T(8,128)(2,1)S(1)} collective-permute-done((bf16[1024,128]{1,0:T(8,128)(2,1)S(1)}, bf16[1024,128]{1,0:T(8,128)(2,1)S(1)}, u32[]{:S(2)}, u32[]{:S(2)}) %collective-permute-start.32) | collective-permute-done | bytes 262176 | tf_op jit(solution)/shard_map/ppermute | solution.py:25
  99.0 1.0 collective-permute-start.36
  100.0 2.1 %collective-permute-start.35 = (bf16[256,512]{1,0:T(8,128)(2,1)S(1)}, bf16[256,512]{1,0:T(8,128)(2,1)S(1)}, u32[]{:S(2)}, u32[]{:S(2)}) collective-permute-start(bf16[256,512]{1,0:T(8,128)(2,1)S(1)} %get-tuple-element.89), channel_id=1, source_target_pairs={{0,64},{32,96},{64,0},{96,32},{128,192},{160,224},{192,128},{224,1... | collective-permute-start | bytes 786440 | tf_op jit(solution)/shard_map/ppermute | solution.py:25
  102.2 1.4 %collective-permute-start.34 = (bf16[256,512]{1,0:T(8,128)(2,1)S(1)}, bf16[256,512]{1,0:T(8,128)(2,1)S(1)}, u32[]{:S(2)}, u32[]{:S(2)}) collective-permute-start(bf16[256,512]{1,0:T(8,128)(2,1)S(1)} %get-tuple-element.89), channel_id=1, source_target_pairs={{0,32},{32,0},{64,96},{96,64},{128,160},{160,128},{192,224},{224,1... | collective-permute-start | bytes 786440 | tf_op jit(solution)/shard_map/ppermute | solution.py:25
  103.6 2.4 %shard_map.94.rest_0_ = bf16[256,8192]{1,0:T(8,128)(2,1)} custom-call(s32[11]{0:T(128)S(1)} %stack.47.where, bf16[256,1536]{1,0:T(8,128)(2,1)S(1)} %get-tuple-element.69.own, bf16[256,1536]{1,0:T(8,128)(2,1)S(1)} %collective-permute-done.18.sib), custom_call_target="tpu_custom_call" | custom-call | bytes 3072 | tf_op jit(solution)/shard_map/pallas_call | solution.py:307
  106.0 1.7 %shard_map.95.rest_0_ = bf16[256,8192]{1,0:T(8,128)(2,1)} custom-call(s32[11]{0:T(128)S(1)} %stack.47.where, bf16[256,1024]{1,0:T(8,128)(2,1)S(1)} %get-tuple-element.67.own, bf16[256,1024]{1,0:T(8,128)(2,1)S(1)} %collective-permute-done.17.sib, bf16[256,8192]{1,0:T(8,128)(2,1)} %shard_map.94.rest_0_), custom_call_target="tpu_custom_call", output_to_operand_aliasing={{}: (3, {})} | custom-call | bytes 2048 | tf_op jit(solution)/shard_map/pallas_call | solution.py:307
  107.7 1.7 %shard_map.96._ = bf16[256,8192]{1,0:T(8,128)(2,1)} custom-call(s32[11]{0:T(128)S(1)} %stack.47.where, bf16[256,1024]{1,0:T(8,128)(2,1)S(1)} %get-tuple-element.65.own, bf16[256,1024]{1,0:T(8,128)(2,1)S(1)} %collective-permute-done.16.sib, bf16[256,8192]{1,0:T(8,128)(2,1)} %shard_map.95.rest_0_), custom_call_target="tpu_custom_call", output_to_operand_aliasing={{}: (3, {})} | custom-call | bytes 2048 | tf_op jit(solution)/shard_map/pallas_call | solution.py:307
  109.4 1.5 %shard_map.97 = (bf16[256,8192]{1,0:T(8,128)(2,1)}, bf16[256,512]{1,0:T(8,128)(2,1)}) custom-call(s32[11]{0:T(128)S(1)} %stack.47.where, bf16[256,512]{1,0:T(8,128)(2,1)S(1)} %get-tuple-element.62.own, bf16[256,1024]{1,0:T(8,128)(2,1)S(1)} %collective-permute-done.15.sib, f32[256,512]{1,0:T(8,128)S(1)} %get-tuple-element.64.total, ...), custom_call_target="tpu_custom_call", output_to_operand_aliasing={{0}: (4, {})} | custom-call | bytes 1024 | tf_op jit(solution)/shard_map/pallas_call | solution.py:307
  110.9 3.2 %collective-permute-done.34.rest_0_ = bf16[256,512]{1,0:T(8,128)(2,1)S(1)} collective-permute-done((bf16[256,512]{1,0:T(8,128)(2,1)S(1)}, bf16[256,512]{1,0:T(8,128)(2,1)S(1)}, u32[]{:S(2)}, u32[]{:S(2)}) %collective-permute-start.34) | collective-permute-done | bytes 262176 | tf_op jit(solution)/shard_map/ppermute | solution.py:25
  114.1 1.5 %shard_map.104 = (bf16[256,512]{1,0:T(8,128)(2,1)}, f32[256,512]{1,0:T(8,128)}) custom-call(s32[11]{0:T(128)S(1)} %stack.47.where, f32[1]{0:T(128)S(6)} %mul.8.rate, bf16[256,512]{1,0:T(8,128)(2,1)S(1)} %bitcast.34, f32[256,512]{1,0:T(8,128)S(1)} %get-tuple-element.87.moved, bf16[256,512]{1,0:T(8,128)(2,1)S(1)} %get-tuple-element.88.other_w, ...), custom_call_target="tpu_custom_call" | custom-call | bytes 3072 | tf_op jit(solution)/shard_map/pallas_call | solution.py:373
  (56 shorter events, 5.7 us)
Async XLA Ops:
  0.6 5.2 %copy-start = (bf16[1,256,512]{2,1,0:T(8,128)(2,1)S(1)}, bf16[1,256,512]{2,1,0:T(8,128)(2,1)}, u32[]{:S(2)}) copy-start(bf16[1,256,512]{2,1,0:T(8,128)(2,1)} %param.8) | copy-start | bytes 786436
  1.7 2.2 %copy-start.1 = (bf16[1,256,8192]{2,1,0:T(8,128)(2,1)S(1)}, bf16[1,256,8192]{2,1,0:T(8,128)(2,1)}, u32[]{:S(2)}) copy-start(bf16[1,256,8192]{2,1,0:T(8,128)(2,1)} %param.5) | copy-start | bytes 12582916
  3.8 2.5 %copy-start.2 = (bf16[1,256,512]{2,1,0:T(8,128)(2,1)S(1)}, bf16[1,256,512]{2,1,0:T(8,128)(2,1)}, u32[]{:S(2)}) copy-start(bf16[1,256,512]{2,1,0:T(8,128)(2,1)} %param.6) | copy-start | bytes 786436
  5.7 9.7 %collective-permute-start.10 = (bf16[256,4096]{1,0:T(8,128)(2,1)S(1)}, bf16[256,4096]{1,0:T(8,128)(2,1)S(1)}, u32[]{:S(2)}, u32[]{:S(2)}) collective-permute-start(bf16[256,4096]{1,0:T(8,128)(2,1)S(1)} %get-tuple-element.54), channel_id=1, source_target_pairs={{0,1},{1,0},{2,3},{3,2},{4,5},{5,4},{6,7},{7,6},{8,9},{9,8},{10,11... | collective-permute-start | bytes 6291464 | tf_op jit(solution)/shard_map/ppermute | solution.py:25
  5.8 9.5 %collective-permute-start.11 = (bf16[256,512]{1,0:T(8,128)(2,1)S(1)}, bf16[256,512]{1,0:T(8,128)(2,1)S(1)}, u32[]{:S(2)}, u32[]{:S(2)}) collective-permute-start(bf16[256,512]{1,0:T(8,128)(2,1)S(1)} %bitcast.20), channel_id=1, source_target_pairs={{0,1},{1,0},{2,3},{3,2},{4,5},{5,4},{6,7},{7,6},{8,9},{9,8},{10,11... | collective-permute-start | bytes 786440 | tf_op jit(solution)/shard_map/ppermute | solution.py:25
  6.3 14.0 %collective-permute-start.2 = (bf16[256,512]{1,0:T(8,128)(2,1)S(1)}, bf16[256,512]{1,0:T(8,128)(2,1)S(1)}, u32[]{:S(2)}, u32[]{:S(2)}) collective-permute-start(bf16[256,512]{1,0:T(8,128)(2,1)S(1)} %bitcast.27), channel_id=1, source_target_pairs={{0,2},{1,3},{2,0},{3,1},{4,6},{5,7},{6,4},{7,5},{8,10},{9,11},{10,... | collective-permute-start | bytes 786440 | tf_op jit(solution)/shard_map/ppermute | solution.py:25
  9.5 11.4 %collective-permute-start.1 = (bf16[256,512]{1,0:T(8,128)(2,1)S(1)}, bf16[256,512]{1,0:T(8,128)(2,1)S(1)}, u32[]{:S(2)}, u32[]{:S(2)}) collective-permute-start(bf16[256,512]{1,0:T(8,128)(2,1)S(1)} %bitcast.28), channel_id=1, source_target_pairs={{0,28},{1,29},{2,30},{3,31},{4,0},{5,1},{6,2},{7,3},{8,4},{9,5},{1... | collective-permute-start | bytes 786440 | tf_op jit(solution)/shard_map/ppermute | solution.py:25
  15.4 9.0 %collective-permute-start = (bf16[256,512]{1,0:T(8,128)(2,1)S(1)}, bf16[256,512]{1,0:T(8,128)(2,1)S(1)}, u32[]{:S(2)}, u32[]{:S(2)}) collective-permute-start(bf16[256,512]{1,0:T(8,128)(2,1)S(1)} %bitcast.29), channel_id=1, source_target_pairs={{0,4},{1,5},{2,6},{3,7},{4,8},{5,9},{6,10},{7,11},{8,12},{9,13},{1... | collective-permute-start | bytes 786440 | tf_op jit(solution)/shard_map/ppermute | solution.py:25
  19.9 9.4 %collective-permute-start.21 = (bf16[1024,128]{1,0:T(8,128)(2,1)S(1)}, bf16[1024,128]{1,0:T(8,128)(2,1)S(1)}, u32[]{:S(2)}, u32[]{:S(2)}) collective-permute-start(bf16[1024,128]{1,0:T(8,128)(2,1)S(1)} %get-tuple-element.76), channel_id=1, source_target_pairs={{0,2},{1,3},{2,0},{3,1},{4,6},{5,7},{6,4},{7,5},{8,10},{9,11},{10,... | collective-permute-start | bytes 786440 | tf_op jit(solution)/shard_map/ppermute | solution.py:25
  25.0 13.3 %collective-permute-start.3 = (bf16[384,512]{1,0:T(8,128)(2,1)S(1)}, bf16[384,512]{1,0:T(8,128)(2,1)S(1)}, u32[]{:S(2)}, u32[]{:S(2)}) collective-permute-start(bf16[384,512]{1,0:T(8,128)(2,1)S(1)} %get-tuple-element.48), channel_id=1, source_target_pairs={{0,4},{1,5},{2,6},{3,7},{4,8},{5,9},{6,10},{7,11},{8,12},{9,13},{1... | collective-permute-start | bytes 1179656 | tf_op jit(solution)/shard_map/ppermute | solution.py:25
  25.0 13.3 %collective-permute-start.5 = (bf16[384,512]{1,0:T(8,128)(2,1)S(1)}, bf16[384,512]{1,0:T(8,128)(2,1)S(1)}, u32[]{:S(2)}, u32[]{:S(2)}) collective-permute-start(bf16[384,512]{1,0:T(8,128)(2,1)S(1)} %get-tuple-element.49), channel_id=1, source_target_pairs={{0,28},{1,29},{2,30},{3,31},{4,0},{5,1},{6,2},{7,3},{8,4},{9,5},{1... | collective-permute-start | bytes 1179656 | tf_op jit(solution)/shard_map/ppermute | solution.py:25
  28.2 10.7 %collective-permute-start.20 = (bf16[1024,128]{1,0:T(8,128)(2,1)S(1)}, bf16[1024,128]{1,0:T(8,128)(2,1)S(1)}, u32[]{:S(2)}, u32[]{:S(2)}) collective-permute-start(bf16[1024,128]{1,0:T(8,128)(2,1)S(1)} %get-tuple-element.75), channel_id=1, source_target_pairs={{0,2},{1,3},{2,0},{3,1},{4,6},{5,7},{6,4},{7,5},{8,10},{9,11},{10,... | collective-permute-start | bytes 786440 | tf_op jit(solution)/shard_map/ppermute | solution.py:25
  29.9 14.0 %collective-permute-start.22 = (bf16[1024,128]{1,0:T(8,128)(2,1)S(1)}, bf16[1024,128]{1,0:T(8,128)(2,1)S(1)}, u32[]{:S(2)}, u32[]{:S(2)}) collective-permute-start(bf16[1024,128]{1,0:T(8,128)(2,1)S(1)} %get-tuple-element.77), channel_id=1, source_target_pairs={{0,4},{1,5},{2,6},{3,7},{4,8},{5,9},{6,10},{7,11},{8,12},{9,13},{1... | collective-permute-start | bytes 786440 | tf_op jit(solution)/shard_map/ppermute | solution.py:25
  29.9 14.0 %collective-permute-start.23 = (bf16[1024,128]{1,0:T(8,128)(2,1)S(1)}, bf16[1024,128]{1,0:T(8,128)(2,1)S(1)}, u32[]{:S(2)}, u32[]{:S(2)}) collective-permute-start(bf16[1024,128]{1,0:T(8,128)(2,1)S(1)} %get-tuple-element.78), channel_id=1, source_target_pairs={{0,28},{1,29},{2,30},{3,31},{4,0},{5,1},{6,2},{7,3},{8,4},{9,5},{1... | collective-permute-start | bytes 786440 | tf_op jit(solution)/shard_map/ppermute | solution.py:25
  38.3 14.0 %collective-permute-start.4 = (bf16[384,512]{1,0:T(8,128)(2,1)S(1)}, bf16[384,512]{1,0:T(8,128)(2,1)S(1)}, u32[]{:S(2)}, u32[]{:S(2)}) collective-permute-start(bf16[384,512]{1,0:T(8,128)(2,1)S(1)} %collective-permute-done.3.refs_0_.refs_4_), channel_id=1, source_target_pairs={{0,4},{1,5},{2,6},{3,7},{4,8},{5,9},{6,10},{7,11},{8,12},{9,13},{1... | collective-permute-start | bytes 1179656 | tf_op jit(solution)/shard_map/ppermute | solution.py:25
  38.3 9.2 %collective-permute-start.28 = (bf16[256,512]{1,0:T(8,128)(2,1)S(1)}, bf16[256,512]{1,0:T(8,128)(2,1)S(1)}, u32[]{:S(2)}, u32[]{:S(2)}) collective-permute-start(bf16[256,512]{1,0:T(8,128)(2,1)S(1)} %bitcast.30), channel_id=1, source_target_pairs={{0,128},{32,160},{64,192},{96,224},{128,0},{160,32},{192,64},{224,... | collective-permute-start | bytes 786440 | tf_op jit(solution)/shard_map/ppermute | solution.py:25
  39.0 8.5 %collective-permute-start.27 = (bf16[256,512]{1,0:T(8,128)(2,1)S(1)}, bf16[256,512]{1,0:T(8,128)(2,1)S(1)}, u32[]{:S(2)}, u32[]{:S(2)}) collective-permute-start(bf16[256,512]{1,0:T(8,128)(2,1)S(1)} %bitcast.31), channel_id=1, source_target_pairs={{0,64},{32,96},{64,0},{96,32},{128,192},{160,224},{192,128},{224,1... | collective-permute-start | bytes 786440 | tf_op jit(solution)/shard_map/ppermute | solution.py:25
  43.9 18.1 %collective-permute-start.19 = (bf16[2560,128]{1,0:T(8,128)(2,1)S(1)}, bf16[2560,128]{1,0:T(8,128)(2,1)S(1)}, u32[]{:S(2)}, u32[]{:S(2)}) collective-permute-start(bf16[2560,128]{1,0:T(8,128)(2,1)S(1)} %get-tuple-element.74), channel_id=1, source_target_pairs={{0,2},{1,3},{2,0},{3,1},{4,6},{5,7},{6,4},{7,5},{8,10},{9,11},{10,... | collective-permute-start | bytes 1966088 | tf_op jit(solution)/shard_map/ppermute | solution.py:25
  43.9 11.5 %collective-permute-start.6 = (bf16[384,512]{1,0:T(8,128)(2,1)S(1)}, bf16[384,512]{1,0:T(8,128)(2,1)S(1)}, u32[]{:S(2)}, u32[]{:S(2)}) collective-permute-start(bf16[384,512]{1,0:T(8,128)(2,1)S(1)} %collective-permute-done.5.refs_1_.refs_5_), channel_id=1, source_target_pairs={{0,28},{1,29},{2,30},{3,31},{4,0},{5,1},{6,2},{7,3},{8,4},{9,5},{1... | collective-permute-start | bytes 1179656 | tf_op jit(solution)/shard_map/ppermute | solution.py:25
  47.5 14.6 %collective-permute-start.24 = (bf16[1536,128]{1,0:T(8,128)(2,1)S(1)}, bf16[1536,128]{1,0:T(8,128)(2,1)S(1)}, u32[]{:S(2)}, u32[]{:S(2)}) collective-permute-start(bf16[1536,128]{1,0:T(8,128)(2,1)S(1)} %get-tuple-element.79), channel_id=1, source_target_pairs={{0,4},{1,5},{2,6},{3,7},{4,8},{5,9},{6,10},{7,11},{8,12},{9,13},{1... | collective-permute-start | bytes 1179656 | tf_op jit(solution)/shard_map/ppermute | solution.py:25
  47.5 14.6 %collective-permute-start.25 = (bf16[1536,128]{1,0:T(8,128)(2,1)S(1)}, bf16[1536,128]{1,0:T(8,128)(2,1)S(1)}, u32[]{:S(2)}, u32[]{:S(2)}) collective-permute-start(bf16[1536,128]{1,0:T(8,128)(2,1)S(1)} %get-tuple-element.80), channel_id=1, source_target_pairs={{0,28},{1,29},{2,30},{3,31},{4,0},{5,1},{6,2},{7,3},{8,4},{9,5},{1... | collective-permute-start | bytes 1179656 | tf_op jit(solution)/shard_map/ppermute | solution.py:25
  52.3 6.4 %collective-permute-start.26 = (bf16[256,512]{1,0:T(8,128)(2,1)S(1)}, bf16[256,512]{1,0:T(8,128)(2,1)S(1)}, u32[]{:S(2)}, u32[]{:S(2)}) collective-permute-start(bf16[256,512]{1,0:T(8,128)(2,1)S(1)} %bitcast.32), channel_id=1, source_target_pairs={{0,32},{32,0},{64,96},{96,64},{128,160},{160,128},{192,224},{224,1... | collective-permute-start | bytes 786440 | tf_op jit(solution)/shard_map/ppermute | solution.py:25
  55.4 11.2 %collective-permute-start.14 = (bf16[256,512]{1,0:T(8,128)(2,1)S(1)}, bf16[256,512]{1,0:T(8,128)(2,1)S(1)}, u32[]{:S(2)}, u32[]{:S(2)}) collective-permute-start(bf16[256,512]{1,0:T(8,128)(2,1)S(1)} %get-tuple-element.58), channel_id=1, source_target_pairs={{0,2},{1,3},{2,0},{3,1},{4,6},{5,7},{6,4},{7,5},{8,10},{9,11},{10,... | collective-permute-start | bytes 786440 | tf_op jit(solution)/shard_map/ppermute | solution.py:25
  58.7 13.6 %collective-permute-start.7 = (bf16[256,512]{1,0:T(8,128)(2,1)S(1)}, bf16[256,512]{1,0:T(8,128)(2,1)S(1)}, u32[]{:S(2)}, u32[]{:S(2)}) collective-permute-start(bf16[256,512]{1,0:T(8,128)(2,1)S(1)} %get-tuple-element.50), channel_id=1, source_target_pairs={{0,4},{1,5},{2,6},{3,7},{4,8},{5,9},{6,10},{7,11},{8,12},{9,13},{1... | collective-permute-start | bytes 786440 | tf_op jit(solution)/shard_map/ppermute | solution.py:25
  62.7 11.6 %collective-permute-start.29 = (bf16[1536,128]{1,0:T(8,128)(2,1)S(1)}, bf16[1536,128]{1,0:T(8,128)(2,1)S(1)}, u32[]{:S(2)}, u32[]{:S(2)}) collective-permute-start(bf16[1536,128]{1,0:T(8,128)(2,1)S(1)} %get-tuple-element.82), channel_id=1, source_target_pairs={{0,4},{1,5},{2,6},{3,7},{4,8},{5,9},{6,10},{7,11},{8,12},{9,13},{1... | collective-permute-start | bytes 1179656 | tf_op jit(solution)/shard_map/ppermute | solution.py:25
  62.7 9.6 %collective-permute-start.8 = (bf16[256,512]{1,0:T(8,128)(2,1)S(1)}, bf16[256,512]{1,0:T(8,128)(2,1)S(1)}, u32[]{:S(2)}, u32[]{:S(2)}) collective-permute-start(bf16[256,512]{1,0:T(8,128)(2,1)S(1)} %get-tuple-element.51), channel_id=1, source_target_pairs={{0,28},{1,29},{2,30},{3,31},{4,0},{5,1},{6,2},{7,3},{8,4},{9,5},{1... | collective-permute-start | bytes 786440 | tf_op jit(solution)/shard_map/ppermute | solution.py:25
  66.0 10.6 %collective-permute-start.30 = (bf16[1536,128]{1,0:T(8,128)(2,1)S(1)}, bf16[1536,128]{1,0:T(8,128)(2,1)S(1)}, u32[]{:S(2)}, u32[]{:S(2)}) collective-permute-start(bf16[1536,128]{1,0:T(8,128)(2,1)S(1)} %get-tuple-element.83), channel_id=1, source_target_pairs={{0,28},{1,29},{2,30},{3,31},{4,0},{5,1},{6,2},{7,3},{8,4},{9,5},{1... | collective-permute-start | bytes 1179656 | tf_op jit(solution)/shard_map/ppermute | solution.py:25
  66.6 11.5 %collective-permute-start.13 = (bf16[256,512]{1,0:T(8,128)(2,1)S(1)}, bf16[256,512]{1,0:T(8,128)(2,1)S(1)}, u32[]{:S(2)}, u32[]{:S(2)}) collective-permute-start(bf16[256,512]{1,0:T(8,128)(2,1)S(1)} %get-tuple-element.57), channel_id=1, source_target_pairs={{0,2},{1,3},{2,0},{3,1},{4,6},{5,7},{6,4},{7,5},{8,10},{9,11},{10,... | collective-permute-start | bytes 786440 | tf_op jit(solution)/shard_map/ppermute | solution.py:25
  72.3 29.9 %collective-permute-start.18 = (bf16[256,1536]{1,0:T(8,128)(2,1)S(1)}, bf16[256,1536]{1,0:T(8,128)(2,1)S(1)}, u32[]{:S(2)}, u32[]{:S(2)}) collective-permute-start(bf16[256,1536]{1,0:T(8,128)(2,1)S(1)} %get-tuple-element.70), channel_id=1, source_target_pairs={{0,1},{1,0},{2,3},{3,2},{4,5},{5,4},{6,7},{7,6},{8,9},{9,8},{10,11... | collective-permute-start | bytes 2359304 | tf_op jit(solution)/shard_map/ppermute | solution.py:25
  72.3 10.7 %collective-permute-start.12 = (bf16[256,512]{1,0:T(8,128)(2,1)S(1)}, bf16[256,512]{1,0:T(8,128)(2,1)S(1)}, u32[]{:S(2)}, u32[]{:S(2)}) collective-permute-start(bf16[256,512]{1,0:T(8,128)(2,1)S(1)} %get-tuple-element.56), channel_id=1, source_target_pairs={{0,2},{1,3},{2,0},{3,1},{4,6},{5,7},{6,4},{7,5},{8,10},{9,11},{10,... | collective-permute-start | bytes 786440 | tf_op jit(solution)/shard_map/ppermute | solution.py:25
  74.3 14.3 %collective-permute-start.9 = (bf16[256,512]{1,0:T(8,128)(2,1)S(1)}, bf16[256,512]{1,0:T(8,128)(2,1)S(1)}, u32[]{:S(2)}, u32[]{:S(2)}) collective-permute-start(bf16[256,512]{1,0:T(8,128)(2,1)S(1)} %get-tuple-element.52), channel_id=1, source_target_pairs={{0,2},{1,3},{2,0},{3,1},{4,6},{5,7},{6,4},{7,5},{8,10},{9,11},{10,... | collective-permute-start | bytes 786440 | tf_op jit(solution)/shard_map/ppermute | solution.py:25
  77.2 13.8 %collective-permute-start.31 = (bf16[1024,128]{1,0:T(8,128)(2,1)S(1)}, bf16[1024,128]{1,0:T(8,128)(2,1)S(1)}, u32[]{:S(2)}, u32[]{:S(2)}) collective-permute-start(bf16[1024,128]{1,0:T(8,128)(2,1)S(1)} %get-tuple-element.84), channel_id=1, source_target_pairs={{0,4},{1,5},{2,6},{3,7},{4,8},{5,9},{6,10},{7,11},{8,12},{9,13},{1... | collective-permute-start | bytes 786440 | tf_op jit(solution)/shard_map/ppermute | solution.py:25
  80.7 19.3 %collective-permute-start.17 = (bf16[256,1024]{1,0:T(8,128)(2,1)S(1)}, bf16[256,1024]{1,0:T(8,128)(2,1)S(1)}, u32[]{:S(2)}, u32[]{:S(2)}) collective-permute-start(bf16[256,1024]{1,0:T(8,128)(2,1)S(1)} %get-tuple-element.68), channel_id=1, source_target_pairs={{0,1},{1,0},{2,3},{3,2},{4,5},{5,4},{6,7},{7,6},{8,9},{9,8},{10,11... | collective-permute-start | bytes 1572872 | tf_op jit(solution)/shard_map/ppermute | solution.py:25
  83.0 8.0 %collective-permute-start.33 = (bf16[512,128]{1,0:T(8,128)(2,1)S(1)}, bf16[512,128]{1,0:T(8,128)(2,1)S(1)}, u32[]{:S(2)}, u32[]{:S(2)}) collective-permute-start(bf16[512,128]{1,0:T(8,128)(2,1)S(1)} %get-tuple-element.86), channel_id=1, source_target_pairs={{0,2},{1,3},{2,0},{3,1},{4,6},{5,7},{6,4},{7,5},{8,10},{9,11},{10,... | collective-permute-start | bytes 393224 | tf_op jit(solution)/shard_map/ppermute | solution.py:25
  86.9 11.9 %copy-start.3 = (f32[1,256,512]{2,1,0:T(8,128)S(1)}, f32[1,256,512]{2,1,0:T(8,128)}, u32[]{:S(2)}) copy-start(f32[1,256,512]{2,1,0:T(8,128)} %param.7) | copy-start | bytes 1572868
  88.6 19.1 %collective-permute-start.16 = (bf16[256,1024]{1,0:T(8,128)(2,1)S(1)}, bf16[256,1024]{1,0:T(8,128)(2,1)S(1)}, u32[]{:S(2)}, u32[]{:S(2)}) collective-permute-start(bf16[256,1024]{1,0:T(8,128)(2,1)S(1)} %get-tuple-element.66), channel_id=1, source_target_pairs={{0,1},{1,0},{2,3},{3,2},{4,5},{5,4},{6,7},{7,6},{8,9},{9,8},{10,11... | collective-permute-start | bytes 1572872 | tf_op jit(solution)/shard_map/ppermute | solution.py:25
  91.0 7.9 %collective-permute-start.32 = (bf16[1024,128]{1,0:T(8,128)(2,1)S(1)}, bf16[1024,128]{1,0:T(8,128)(2,1)S(1)}, u32[]{:S(2)}, u32[]{:S(2)}) collective-permute-start(bf16[1024,128]{1,0:T(8,128)(2,1)S(1)} %get-tuple-element.85), channel_id=1, source_target_pairs={{0,28},{1,29},{2,30},{3,31},{4,0},{5,1},{6,2},{7,3},{8,4},{9,5},{1... | collective-permute-start | bytes 786440 | tf_op jit(solution)/shard_map/ppermute | solution.py:25
  91.0 18.4 %collective-permute-start.15 = (bf16[256,1024]{1,0:T(8,128)(2,1)S(1)}, bf16[256,1024]{1,0:T(8,128)(2,1)S(1)}, u32[]{:S(2)}, u32[]{:S(2)}) collective-permute-start(bf16[256,1024]{1,0:T(8,128)(2,1)S(1)} %get-tuple-element.63), channel_id=1, source_target_pairs={{0,1},{1,0},{2,3},{3,2},{4,5},{5,4},{6,7},{7,6},{8,9},{9,8},{10,11... | collective-permute-start | bytes 1572872 | tf_op jit(solution)/shard_map/ppermute | solution.py:25
  99.0 11.9 %collective-permute-start.36 = (bf16[256,512]{1,0:T(8,128)(2,1)S(1)}, bf16[256,512]{1,0:T(8,128)(2,1)S(1)}, u32[]{:S(2)}, u32[]{:S(2)}) collective-permute-start(bf16[256,512]{1,0:T(8,128)(2,1)S(1)} %get-tuple-element.89), channel_id=1, source_target_pairs={{0,128},{32,160},{64,192},{96,224},{128,0},{160,32},{192,64},{224,... | collective-permute-start | bytes 786440 | tf_op jit(solution)/shard_map/ppermute | solution.py:25
  100.0 10.9 %collective-permute-start.35 = (bf16[256,512]{1,0:T(8,128)(2,1)S(1)}, bf16[256,512]{1,0:T(8,128)(2,1)S(1)}, u32[]{:S(2)}, u32[]{:S(2)}) collective-permute-start(bf16[256,512]{1,0:T(8,128)(2,1)S(1)} %get-tuple-element.89), channel_id=1, source_target_pairs={{0,64},{32,96},{64,0},{96,32},{128,192},{160,224},{192,128},{224,1... | collective-permute-start | bytes 786440 | tf_op jit(solution)/shard_map/ppermute | solution.py:25
  102.2 12.0 %collective-permute-start.34 = (bf16[256,512]{1,0:T(8,128)(2,1)S(1)}, bf16[256,512]{1,0:T(8,128)(2,1)S(1)}, u32[]{:S(2)}, u32[]{:S(2)}) collective-permute-start(bf16[256,512]{1,0:T(8,128)(2,1)S(1)} %get-tuple-element.89), channel_id=1, source_target_pairs={{0,32},{32,0},{64,96},{96,64},{128,160},{160,128},{192,224},{224,1... | collective-permute-start | bytes 786440 | tf_op jit(solution)/shard_map/ppermute | solution.py:25
